TPU v7x, 256 devices: a whole 4x4x8 slice. The times are simulated.
256 devices in a mesh: ctx: 32 (over z, y), head: 8 (over x, core).
Axes of the slice: x: 4, y: 4, z: 8, core: 2. Of those that a mesh axis runs over, the one named last changes fastest.
Arguments:
- q_latent: bfloat16 [4096, 32768], P('ctx', 'head'), may hold values from -48 to 48
- q_rope: bfloat16 [4096, 4096], P('ctx', 'head'), may hold values from -6 to 6
- out_grad: bfloat16 [4096, 32768], P('ctx', 'head'), may hold values from -6 to 6
- kv_latent: bfloat16 [128, 128, 512], P('ctx'), may hold values from -6 to 6
- key_rope: bfloat16 [128, 64, 128], P('ctx'), may hold values from -6 to 6
- block_lists: int32 [4096, 16], P('ctx'), may hold values from -1 to 127, as said below
- query_pos: int32 [4096], P('ctx'), may hold values from 0 to 16383, as said below
Outputs:
- dq_latent: bfloat16 [4096, 32768], P('ctx', 'head')
- dq_rope: bfloat16 [4096, 4096], P('ctx', 'head')
- dkv_latent: float32 [128, 128, 512], P('ctx', 'head')
- dkey_rope: float32 [128, 64, 128], P('ctx', 'head')
Inputs may be any that keep to these rules, and one draw needn't show every extreme that they name: `query_pos`: query i of the queries held by index c of ctx (rows c * 128 to (c + 1) * 128 - 1) stands at a position of that index's own keys, c * 512 to (c + 1) * 512 - 1. `block_lists`: each row names distinct blocks: first the blocks of the same index of ctx, in ascending order from that index's first block up to and including its own query's block, then blocks of earlier indices of ctx only, then -1. Over the 128 rows of one index of ctx, at most 1 distinct block of any one other index is named, and at most 13 distinct blocks of other indices in all; both bounds are reached on every index that has 13 or more earlier indices. Every index of ctx from 1 on names a block of index 0 other than block 0.
All inputs are finite; a program needn't handle non-finite values.
Results may differ from a plain program's by a relative error of at most 0.013.
Values may be sent and summed in bfloat16 or wider, within the bound.
No kernel may reach another device: no remote copies, remote signals or barrier semaphores. Data moves between devices by JAX's collectives and lax.ppermute only.
A program may use at most 128 MiB of HBM per device.

v0:
```python
import functools

import jax
import jax.numpy as jnp
from jax import lax
from jax.experimental import pallas as pl
from jax.experimental.pallas import tpu as pltpu
from jax.sharding import PartitionSpec as P

SCALE_FACTOR = 192.0 ** (-0.5)
LOG2E = 1.4426950408889634
NEG_FILL = -1e30
BF = jnp.bfloat16
F32 = jnp.float32
LAT = 512
WIDE = 640
SHARE = 16
REMOTE = 13
OWN = 4
FAR_ROWS = REMOTE * SHARE
GROUP = (REMOTE + OWN) * SHARE
GROUPS = 8
KEYS = GROUP * GROUPS
CHIP = 2 * GROUP
HEADS = 8
ROWS = 1024
CH = 256
NCH = ROWS // CH
SPAN = OWN * SHARE
SLOTS = 32
NZ, NY, NX = 8, 4, 4


def params(mib):
    return pltpu.CompilerParams(vmem_limit_bytes=mib * 1024 * 1024)


def after(x, *deps):
    return lax.optimization_barrier((x,) + deps)[0]


def cost(flops, nbytes):
    return pl.CostEstimate(flops=flops, bytes_accessed=nbytes, transcendentals=0)


def vspec():
    return pl.BlockSpec(memory_space=pltpu.VMEM)


def hbm_spec():
    return pl.BlockSpec(memory_space=pltpu.HBM)


def nt_dot(a, b):
    return lax.dot_general(a, b, (((1,), (1,)), ((), ())), preferred_element_type=F32)


def tn_dot(a, b):
    return lax.dot_general(a, b, (((0,), (0,)), ((), ())), preferred_element_type=F32)


def unpack_rope(packed, core):
    row = lax.broadcasted_iota(jnp.int32, (SHARE, SHARE), 0)
    col = lax.broadcasted_iota(jnp.int32, (SHARE, SHARE), 1)
    pick = jnp.where(col == core * 8 + row // 2, 1.0, 0.0).astype(BF)
    wide = jnp.dot(pick, packed, preferred_element_type=F32)
    lane = lax.broadcasted_iota(jnp.int32, (SHARE, 128), 1)
    odd = lax.broadcasted_iota(jnp.int32, (SHARE, 128), 0) % 2 == 1
    both = jnp.where(odd, pltpu.roll(wide, 64, 1), wide)
    return jnp.where(lane < 64, both, 0.0).astype(BF)


def pack_body(kv_ref, rope_ref, out_ref, lat, rope, sems):
    head = lax.axis_index("head")
    wide = kv_ref.at[:, pl.ds(pl.multiple_of(head * SHARE, SHARE), SHARE), :]
    thin = rope_ref.at[:, pl.ds(pl.multiple_of(head // 2 * SHARE, SHARE), SHARE), :]
    copies = (
        pltpu.make_async_copy(wide, lat, sems.at[0]),
        pltpu.make_async_copy(thin, rope, sems.at[1]),
    )
    for copy in copies:
        copy.start()
    for copy in copies:
        copy.wait()
    for b in range(OWN):
        thin_rows = unpack_rope(rope[b], head % 2)
        for z in range(NZ):
            rows = slice(z * SPAN + b * SHARE, z * SPAN + (b + 1) * SHARE)
            out_ref[rows, :LAT] = lat[b]
            out_ref[rows, LAT:] = thin_rows


def pack_call(kv, rope):
    return pl.pallas_call(
        pack_body,
        in_specs=[hbm_spec()] * 2,
        out_specs=vspec(),
        out_shape=jax.ShapeDtypeStruct((NZ * SPAN, WIDE), BF),
        scratch_shapes=[
            pltpu.VMEM((OWN, SHARE, LAT), BF),
            pltpu.VMEM((OWN, SHARE, 128), BF),
            pltpu.SemaphoreType.DMA((2,)),
        ],
        compiler_params=params(56),
        name="pack_share",
    )(kv, rope)


def share_of(me, g):
    return (me // 2 + NX - g // 2) % NX, (me % 2 + g % 2) % 2


def prep_body(kv_hbm, rope_hbm, q_hbm, qr_hbm, g_hbm, own_out, q_out, g_out,
              kv_ref, rope_ref, qr_ref, sems):
    copies = [
        pltpu.make_async_copy(qr_hbm, qr_ref, sems.at[0]),
        pltpu.make_async_copy(rope_hbm, rope_ref, sems.at[1]),
        pltpu.make_async_copy(kv_hbm, kv_ref, sems.at[2]),
    ]
    for h in range(HEADS):
        cols, rows = pl.ds(h * LAT, LAT), pl.ds(h * 128, 128)
        copies.append(pltpu.make_async_copy(
            q_hbm.at[:, cols], q_out.at[rows, pl.ds(0, LAT)], sems.at[3 + 2 * h]))
        copies.append(pltpu.make_async_copy(
            g_hbm.at[:, cols], g_out.at[rows, :], sems.at[4 + 2 * h]))
    for copy in copies:
        copy.start()
    me = lax.axis_index("head")
    lane = lax.broadcasted_iota(jnp.int32, (128, 128), 1)
    copies[0].wait()
    for h in range(HEADS):
        pair = qr_ref[:, (h // 2) * 128:(h // 2 + 1) * 128].astype(F32)
        if h % 2:
            pair = pltpu.roll(pair, 64, 1)
        q_out[h * 128:(h + 1) * 128, LAT:] = jnp.where(lane < 64, pair, 0.0).astype(BF)
    copies[1].wait()
    for g in range(GROUPS):
        chip, core = share_of(me, g)
        for b in range(OWN):
            own_out[g, b * SHARE:(b + 1) * SHARE, LAT:] = unpack_rope(
                rope_ref[b, pl.ds(pl.multiple_of(chip * SHARE, SHARE), SHARE), :], core
            )
    copies[2].wait()
    for g in range(GROUPS):
        chip, core = share_of(me, g)
        at = pl.multiple_of((chip * 2 + core) * SHARE, SHARE)
        for b in range(OWN):
            own_out[g, b * SHARE:(b + 1) * SHARE, :LAT] = kv_ref[b, pl.ds(at, SHARE), :]
    for copy in copies[3:]:
        copy.wait()


def prep_call(kv, rope, q, qr, g):
    return pl.pallas_call(
        prep_body,
        in_specs=[hbm_spec()] * 5,
        out_specs=[vspec()] * 3,
        out_shape=[
            jax.ShapeDtypeStruct((GROUPS, SPAN, WIDE), BF),
            jax.ShapeDtypeStruct((ROWS, WIDE), BF),
            jax.ShapeDtypeStruct((ROWS, LAT), BF),
        ],
        scratch_shapes=[
            pltpu.VMEM(kv.shape, BF),
            pltpu.VMEM(rope.shape, BF),
            pltpu.VMEM(qr.shape, BF),
            pltpu.SemaphoreType.DMA((3 + 2 * HEADS,)),
        ],
        compiler_params=params(10),
        cost_estimate=cost(1000, 10_000_000),
        name="prep_operands",
    )(kv, rope, q, qr, g)


def pick_y_body(*refs):
    wants, shards, outs = refs[:NY], refs[NY], refs[NY + 1:]
    ctx = lax.axis_index("ctx")
    for r in range(NZ):
        z = (ctx // NY + NZ - r) % NZ
        for dy in range(NY):
            w = jnp.maximum(wants[dy][z * NY + ctx % NY], 0)
            at = pl.multiple_of((z * OWN + w) * SHARE, SHARE)
            outs[dy][r * SHARE:(r + 1) * SHARE, :] = shards[pl.ds(at, SHARE), :]


def pick_y_call(wants, shards):
    return pl.pallas_call(
        pick_y_body,
        in_specs=[pl.BlockSpec(memory_space=pltpu.SMEM)] * NY + [vspec()],
        out_specs=[vspec()] * NY,
        out_shape=[jax.ShapeDtypeStruct((NZ * SHARE, WIDE), BF)] * NY,
        compiler_params=params(4),
        name="pick_for_y_peers",
    )(*wants, shards)


def pick_x_body(src_ref, y0, y1, y2, y3, out_ref, stage):
    span = NZ * SHARE
    for dy, ref in enumerate((y0, y1, y2, y3)):
        stage[dy * span:(dy + 1) * span, :] = ref[...]
    for u in range(REMOTE):
        at = pl.multiple_of(src_ref[u] * SHARE, SHARE)
        out_ref[u * SHARE:(u + 1) * SHARE, :] = stage[pl.ds(at, SHARE), :]


def pick_x_call(src, cols):
    return pl.pallas_call(
        pick_x_body,
        in_specs=[pl.BlockSpec(memory_space=pltpu.SMEM)] + [vspec()] * NY,
        out_specs=vspec(),
        out_shape=jax.ShapeDtypeStruct((FAR_ROWS, WIDE), BF),
        scratch_shapes=[pltpu.VMEM((NY * NZ * SHARE, WIDE), BF)],
        compiler_params=params(4),
        name="pick_selected",
    )(src, *cols)


def scores_body(me_ref, far_ref, pos_ref, x0, x1, x2, x3, c0, c1, c2, c3, own, q_ref, g_ref,
                k_out, p_out, ds_out, s_scr, e_scr, bias_scr):
    me = me_ref[0]
    pos = pos_ref[...] - me_ref[1]
    for u in range(REMOTE):
        line = jnp.broadcast_to(far_ref[u:u + 1, :], (SHARE, 128))
        for g in range(GROUPS):
            bias_scr[g * GROUP + u * SHARE:g * GROUP + (u + 1) * SHARE, :] = line
    step = lax.broadcasted_iota(jnp.int32, (SHARE, 128), 0)
    for g in range(GROUPS):
        chip, core = share_of(me, g)
        for b in range(OWN):
            at = g * GROUP + FAR_ROWS + b * SHARE
            key = step + (b * 128 + (chip * 2 + core) * SHARE)
            bias_scr[at:at + SHARE, :] = jnp.where(key <= pos, 0.0, NEG_FILL)
    for g, ref in enumerate((x0, c0, x1, c1, x2, c2, x3, c3)):
        k_out[g * GROUP:g * GROUP + FAR_ROWS, :] = ref[...]
        k_out[g * GROUP + FAR_ROWS:(g + 1) * GROUP, :] = own[g]

    def chunk(c, carry):
        at = c * CH
        q = q_ref[pl.ds(at, CH), :]
        g = g_ref[pl.ds(at, CH), :]
        top = jnp.full((1, CH), -jnp.inf, F32)
        for k in range(GROUPS):
            rows = slice(k * GROUP, (k + 1) * GROUP)
            bias = bias_scr[rows, :]
            s = nt_dot(k_out[rows, :], q) * (SCALE_FACTOR * LOG2E)
            s = s + jnp.concatenate([bias, bias], axis=1)
            s_scr[rows, :] = s
            top = jnp.maximum(top, jnp.max(s, axis=0, keepdims=True))
        total = jnp.zeros((1, CH), F32)
        delta = jnp.zeros((1, CH), F32)
        for k in range(GROUPS):
            rows = slice(k * GROUP, (k + 1) * GROUP)
            e = nt_dot(k_out[rows, :LAT], g)
            e_scr[rows, :] = e
            w = jnp.exp2(s_scr[rows, :] - top)
            s_scr[rows, :] = w
            total = total + jnp.sum(w, axis=0, keepdims=True)
            delta = delta + jnp.sum(w * e, axis=0, keepdims=True)
        inv = 1.0 / total
        delta = delta * inv
        for k in range(GROUPS):
            rows = slice(k * GROUP, (k + 1) * GROUP)
            p = s_scr[rows, :] * inv
            p_out[c, rows, :] = p.astype(BF)
            ds_out[c, rows, :] = ((e_scr[rows, :] - delta) * (p * SCALE_FACTOR)).astype(BF)
        return carry

    for c in range(NCH):
        chunk(c, 0)


def scores_call(me, far, pos, xs, cs, own, q, g):
    return pl.pallas_call(
        scores_body,
        in_specs=[pl.BlockSpec(memory_space=pltpu.SMEM)] + [vspec()] * 13,
        out_specs=[vspec()] * 3,
        out_shape=[
            jax.ShapeDtypeStruct((KEYS, WIDE), BF),
            jax.ShapeDtypeStruct((NCH, KEYS, CH), BF),
            jax.ShapeDtypeStruct((NCH, KEYS, CH), BF),
        ],
        scratch_shapes=[
            pltpu.VMEM((KEYS, CH), F32),
            pltpu.VMEM((KEYS, CH), F32),
            pltpu.VMEM((KEYS, 128), F32),
        ],
        compiler_params=params(30),
        cost_estimate=cost(2 * KEYS * ROWS * 1152, 16_000_000),
        name="scores",
    )(me, far, pos, *xs, *cs, own, q, g)


def dkv_body(p_ref, ds_ref, q_ref, g_ref, keep_ref, send_ref):
    for cr, out in enumerate((keep_ref, send_ref)):
        rows = slice(cr * GROUP, (cr + 1) * GROUP)
        ds = jnp.concatenate([ds_ref[c, rows, :] for c in range(NCH)], axis=1)
        p = jnp.concatenate([p_ref[c, rows, :] for c in range(NCH)], axis=1)
        a = jnp.dot(ds, q_ref[...], preferred_element_type=F32)
        b = jnp.dot(p, g_ref[...], preferred_element_type=F32)
        out[:, :LAT] = (a[:, :LAT] + b).astype(out.dtype)
        out[:, LAT:] = a[:, LAT:].astype(out.dtype)


def dkv_call(dx, p, ds, q, g):
    part = pl.BlockSpec((NCH, CHIP, CH), lambda i: (0, dx, 0))
    return pl.pallas_call(
        dkv_body,
        grid=(1,),
        in_specs=[part, part, pl.BlockSpec((ROWS, WIDE), lambda i: (0, 0)),
                  pl.BlockSpec((ROWS, LAT), lambda i: (0, 0))],
        out_specs=[pl.BlockSpec((GROUP, WIDE), lambda i: (0, 0))] * 2,
        out_shape=[
            jax.ShapeDtypeStruct((GROUP, WIDE), F32),
            jax.ShapeDtypeStruct((GROUP, WIDE), BF),
        ],
        compiler_params=params(16),
        cost_estimate=cost(2 * CHIP * ROWS * 1152, 5_000_000),
        name=f"dkv_chunk{dx}",
    )(p, ds, q, g)


def dq_body(ds_ref, k_ref, lat_ref, rope_ref):
    res = tn_dot(ds_ref[0], k_ref[...])
    lat_ref[:, :LAT] = res[:128, :LAT].astype(BF)
    lat_ref[:, LAT:] = res[128:, :LAT].astype(BF)
    lane = lax.broadcasted_iota(jnp.int32, (128, 128), 1)
    odd = pltpu.roll(res[128:, LAT:], 64, 1)
    rope_ref[...] = jnp.where(lane < 64, res[:128, LAT:], odd).astype(BF)


def dq_call(ds, keys):
    return pl.pallas_call(
        dq_body,
        grid=(NCH,),
        in_specs=[
            pl.BlockSpec((1, KEYS, CH), lambda i: (i, 0, 0)),
            pl.BlockSpec((KEYS, WIDE), lambda i: (0, 0)),
        ],
        out_specs=[
            pl.BlockSpec((128, 2 * LAT), lambda i: (0, i)),
            pl.BlockSpec((128, 128), lambda i: (0, i)),
        ],
        out_shape=[
            jax.ShapeDtypeStruct((128, HEADS * LAT), BF),
            jax.ShapeDtypeStruct((128, HEADS * 64), BF),
        ],
        compiler_params=params(14),
        cost_estimate=cost(2 * KEYS * ROWS * 640, 8_000_000),
        name="dq",
    )(ds, keys)


def slots_body(at_ref, want_ref, keep_ref, swap_ref, r1_ref, r2_ref, r3_ref,
               slot_out, own_out, far):
    total = keep_ref[...] + swap_ref[...].astype(F32)
    for ref in (r1_ref, r2_ref, r3_ref):
        total = total + ref[...].astype(F32)
    own_out[...] = total[FAR_ROWS:, :]
    far[...] = total[:FAR_ROWS, :]
    lane = lax.broadcasted_iota(jnp.int32, (SHARE, 128), 1)
    for c in range(SLOTS):
        rows = slice(c * SHARE, (c + 1) * SHARE)
        w = want_ref[c]
        flag = jnp.where(w >= 0, 64 + w, 128)
        piece = far[pl.ds(pl.multiple_of(at_ref[c] * SHARE, SHARE), SHARE), :]
        slot_out[rows, :LAT] = piece[:, :LAT].astype(BF)
        slot_out[rows, LAT:] = jnp.where(lane == flag, 1.0, piece[:, LAT:]).astype(BF)


def slots_call(at, want, keep, swap, r1, r2, r3):
    smem = pl.BlockSpec(memory_space=pltpu.SMEM)
    return pl.pallas_call(
        slots_body,
        in_specs=[smem, smem] + [vspec()] * 5,
        out_specs=[vspec()] * 2,
        out_shape=[
            jax.ShapeDtypeStruct((SLOTS * SHARE, WIDE), BF),
            jax.ShapeDtypeStruct((SPAN, WIDE), F32),
        ],
        scratch_shapes=[pltpu.VMEM((FAR_ROWS, WIDE), F32)],
        compiler_params=params(8),
        name="fill_slots",
    )(at, want, keep, swap, r1, r2, r3)


def finish_body(own_ref, back_ref, lat_ref, rope_ref, acc, scr):
    acc[...] = own_ref[...]
    for c in range(SLOTS):
        piece = back_ref[c * SHARE:(c + 1) * SHARE, :].astype(F32)
        for b in range(OWN):
            mine = piece[:, LAT + 64 + b:LAT + 65 + b] > 0.5
            acc[b * SHARE:(b + 1) * SHARE, :] += jnp.where(mine, piece, 0.0)
    for b in range(OWN):
        lat_ref[b] = acc[b * SHARE:(b + 1) * SHARE, :LAT]
    scr[...] = acc[:, LAT:]
    half = SPAN // 2
    even = scr[pl.ds(0, half, 2), :]
    odd = scr[pl.ds(1, half, 2), :]
    lane = lax.broadcasted_iota(jnp.int32, (half, 128), 1)
    both = jnp.where(lane < 64, even, pltpu.roll(odd, 64, 1))
    rope_ref[...] = both.reshape(OWN, SHARE // 2, 128)


def finish_call(own, back):
    return pl.pallas_call(
        finish_body,
        in_specs=[vspec()] * 2,
        out_specs=[vspec()] * 2,
        out_shape=[
            jax.ShapeDtypeStruct((OWN, SHARE, LAT), F32),
            jax.ShapeDtypeStruct((OWN, SHARE // 2, 128), F32),
        ],
        scratch_shapes=[pltpu.VMEM((SPAN, WIDE), F32), pltpu.VMEM((SPAN, 128), F32)],
        compiler_params=params(8),
        name="finish",
    )(own, back)


def step_z(a, d):
    return lax.ppermute(a, "ctx", [(i, (i + NY * d) % (NZ * NY)) for i in range(NZ * NY)])


def step_y(a, d):
    return lax.ppermute(
        a, "ctx", [(z * NY + y, z * NY + (y + d) % NY) for z in range(NZ) for y in range(NY)]
    )


def step_x(a, d):
    return lax.ppermute(a, "head", [(i, (i + 2 * d) % (2 * NX)) for i in range(2 * NX)])


def swap_core(a):
    return lax.ppermute(a, "head", [(i, i ^ 1) for i in range(2 * NX)])


def local(q_latent, q_rope, out_grad, kv_latent, key_rope, block_lists, query_pos):
    ctx = lax.axis_index("ctx")
    head = lax.axis_index("head")
    my_z, my_y = ctx // NY, ctx % NY
    me = jnp.stack([head, ctx * (OWN * 128)]).astype(jnp.int32)

    shard = pack_call(kv_latent, key_rope)
    columns = [[z * NY + y for z in range(NZ)] for y in range(NY)]
    shards = lax.all_to_all(shard, "ctx", 0, 0, tiled=True, axis_index_groups=columns)

    block_lists, me, query_pos = after((block_lists, me, query_pos), shard)
    every = jnp.arange(NZ * NY * OWN, dtype=jnp.int32)
    present = jnp.any(block_lists.reshape(-1)[:, None] == every[None, :], axis=0)
    remote = present & (every // OWN != ctx)
    grid = remote.reshape(NZ * NY, OWN)
    want = jnp.max(jnp.where(grid, jnp.arange(OWN, dtype=jnp.int32)[None, :], -1), axis=1)
    rank = jnp.cumsum(remote.astype(jnp.int32)) - 1
    slot_ids = jnp.arange(16, dtype=jnp.int32)
    match = remote[None, :] & (rank[None, :] == slot_ids[:, None])
    remote_ids = jnp.max(jnp.where(match, every[None, :], -1), axis=1)
    owner = jnp.maximum(remote_ids, 0) // OWN
    src = jnp.where(
        remote_ids >= 0, ((my_y - owner % NY) % NY) * NZ + (my_z - owner // NY) % NZ, 0
    ).astype(jnp.int32)
    ctxs = jnp.arange(SLOTS, dtype=jnp.int32)
    hit = (remote_ids[None, :] >= 0) & (remote_ids[None, :] // OWN == ctxs[:, None])
    back_at = jnp.sum(jnp.where(hit, slot_ids[None, :], 0), axis=1).astype(jnp.int32)
    wants = [want] + [step_y(want, -d) for d in range(1, NY)]
    chosen = jnp.any(block_lists[:, None, :] == remote_ids[None, :, None], axis=2)
    chosen = chosen & (remote_ids >= 0)[None, :]
    far_bias = jnp.where(chosen, 0.0, NEG_FILL).astype(F32).T

    cols = pick_y_call(wants, shards)
    cols = [cols[0]] + [step_y(cols[d], d) for d in range(1, NY)]
    x0 = pick_x_call(src, cols)
    x2, x1, x3 = step_x(x0, 2), step_x(x0, 1), step_x(x0, -1)
    xs = [x0, x1, x2, x3]
    arrays = after((kv_latent, key_rope, q_latent, q_rope, out_grad), x0)
    own_keys, q, g = prep_call(*arrays)
    cs = [swap_core(x0)] + [swap_core(after(a, own_keys)) for a in xs[1:]]

    keys, p, ds = scores_call(me, far_bias, query_pos.reshape(1, -1), xs, cs, own_keys, q, g)

    order = (2, 1, 3, 0)
    keep, send, part, got = {}, {}, {}, {}
    for n, dx in enumerate(order):
        keep[dx], send[dx] = dkv_call(dx, p, ds, q, g)
        p, ds = after((p, ds), send[dx])
        if n:
            prev = order[n - 1]
            part[prev] = (keep[prev] + swap_core(send[prev]).astype(F32)).astype(BF)
            got[prev] = step_x(part[prev], -prev)
            p, ds = after((p, ds), part[prev])
    swap = swap_core(send[0])
    dq_latent, dq_rope = dq_call(ds, keys)
    mine, dq_latent, dq_rope = lax.optimization_barrier((keep[0], dq_latent, dq_rope))

    slots, own = slots_call(back_at, want, mine, swap, got[1], got[2], got[3])
    back = lax.all_to_all(slots, "ctx", split_axis=0, concat_axis=0, tiled=True)
    dkv_latent, dkey_rope = finish_call(own, back)
    return (dq_latent, dq_rope, dkv_latent, dkey_rope)


def solution(mesh):
    return jax.shard_map(
        local,
        mesh=mesh,
        in_specs=(
            P("ctx", "head"),
            P("ctx", "head"),
            P("ctx", "head"),
            P("ctx", None, None),
            P("ctx", None, None),
            P("ctx", None),
            P("ctx"),
        ),
        out_specs=(
            P("ctx", "head"),
            P("ctx", "head"),
            P("ctx", "head", None),
            P("ctx", "head", None),
        ),
        check_vma=False,
    )
```

profile of v0, /device:TPU:8, one launch (start us, length us, event | category | flops | bytes accessed | tf_op | source)
XLA Modules:
  0.0 123.8 jit_solution(6163180632752478338)
XLA Ops:
  0.7 2.1 %pack_share.1 = bf16[512,640]{1,0:T(8,128)(2,1)} custom-call(bf16[4,128,512]{2,1,0:T(8,128)(2,1)} %kv_hbm, bf16[4,64,128]{2,1,0:T(8,128)(2,1)} %rope_hbm), custom_call_target="tpu_custom_call" | custom-call | tf_op jit(solution)/shard_map/pack_share/pallas_call | solution.py:94
  2.8 8.5 %all-to-all-start = ((bf16[8,64,640]{2,1,0:T(8,128)(2,1)}), bf16[8,64,640]{2,1,0:T(8,128)(2,1)S(1)}, u32[]{:S(2)}, u32[]{:S(2)}) async-start(bf16[8,64,640]{2,1,0:T(8,128)(2,1)} %bitcast.14), calls=%async_computation | async-start | bytes 1310720 | tf_op jit(solution)/shard_map/all_to_all | solution.py:445
  14.1 1.7 %collective-permute-start.2 = (s32[32]{0:T(128)S(1)}, s32[32]{0:T(128)S(1)}, u32[]{:S(2)}, u32[]{:S(2)}) collective-permute-start(s32[32]{0:T(128)S(1)} %select_reduce_fusion.refs_0_.want_ref), channel_id=1, source_target_pairs={{0,8},{8,16},{16,24},{24,0},{32,40},{40,48},{48,56},{56,32},{64,72... | collective-permute-start | bytes 392 | tf_op jit(solution)/shard_map/ppermute | solution.py:424
  16.7 2.4 %collective-permute-start = (s32[32]{0:T(128)S(1)}, s32[32]{0:T(128)S(1)}, u32[]{:S(2)}, u32[]{:S(2)}) collective-permute-start(s32[32]{0:T(128)S(1)} %select_reduce_fusion.refs_0_.want_ref), channel_id=1, source_target_pairs={{0,24},{8,0},{16,8},{24,16},{32,56},{40,32},{48,40},{56,48},{64,88... | collective-permute-start | bytes 392 | tf_op jit(solution)/shard_map/ppermute | solution.py:424
  19.9 1.6 %reduce-window.8 = s32[128,1]{1,0:T(8,128)} reduce-window(s32[128,1]{1,0:T(8,128)} %fusion.6, s32[]{:T(128)} %constant.117.clone.1), window={size=128x1 pad=127_0x0_0}, to_apply=%region_1.2 | reduce-window | flops 16256 | bytes 1028 | tf_op jit(solution)/shard_map/reduce-window.3
  22.6 8.9 %all-to-all-done = bf16[8,64,640]{2,1,0:T(8,128)(2,1)S(1)} async-done(((bf16[8,64,640]{2,1,0:T(8,128)(2,1)}), bf16[8,64,640]{2,1,0:T(8,128)(2,1)S(1)}, u32[]{:S(2)}, u32[]{:S(2)}) %all-to-all-start) | async-done | bytes 655392 | tf_op jit(solution)/shard_map/all_to_all | solution.py:445
  32.2 1.7 %collective-permute-start.3 = (bf16[128,640]{1,0:T(8,128)(2,1)S(1)}, bf16[128,640]{1,0:T(8,128)(2,1)S(1)}, u32[]{:S(2)}, u32[]{:S(2)}) collective-permute-start(bf16[128,640]{1,0:T(8,128)(2,1)S(1)} %get-tuple-element.58), channel_id=1, source_target_pairs={{0,8},{8,16},{16,24},{24,0},{32,40},{40,48},{48,56},{56,32},{64,72... | collective-permute-start | bytes 491528 | tf_op jit(solution)/shard_map/ppermute | solution.py:424
  34.8 2.4 %collective-permute-start.5 = (bf16[128,640]{1,0:T(8,128)(2,1)S(1)}, bf16[128,640]{1,0:T(8,128)(2,1)S(1)}, u32[]{:S(2)}, u32[]{:S(2)}) collective-permute-start(bf16[128,640]{1,0:T(8,128)(2,1)S(1)} %get-tuple-element.60), channel_id=1, source_target_pairs={{0,24},{8,0},{16,8},{24,16},{32,56},{40,32},{48,40},{56,48},{64,88... | collective-permute-start | bytes 491528 | tf_op jit(solution)/shard_map/ppermute | solution.py:424
  37.3 2.0 %collective-permute-done.3.y1 = bf16[128,640]{1,0:T(8,128)(2,1)S(1)} collective-permute-done((bf16[128,640]{1,0:T(8,128)(2,1)S(1)}, bf16[128,640]{1,0:T(8,128)(2,1)S(1)}, u32[]{:S(2)}, u32[]{:S(2)}) %collective-permute-start.3) | collective-permute-done | bytes 163872 | tf_op jit(solution)/shard_map/ppermute | solution.py:424
  39.3 3.2 %collective-permute-done.4.y2 = bf16[128,640]{1,0:T(8,128)(2,1)S(1)} collective-permute-done((bf16[128,640]{1,0:T(8,128)(2,1)S(1)}, bf16[128,640]{1,0:T(8,128)(2,1)S(1)}, u32[]{:S(2)}, u32[]{:S(2)}) %collective-permute-start.4) | collective-permute-done | bytes 163872 | tf_op jit(solution)/shard_map/ppermute | solution.py:424
  42.5 1.6 %collective-permute-done.5.y3 = bf16[128,640]{1,0:T(8,128)(2,1)S(1)} collective-permute-done((bf16[128,640]{1,0:T(8,128)(2,1)S(1)}, bf16[128,640]{1,0:T(8,128)(2,1)S(1)}, u32[]{:S(2)}, u32[]{:S(2)}) %collective-permute-start.5) | collective-permute-done | bytes 163872 | tf_op jit(solution)/shard_map/ppermute | solution.py:424
  44.7 2.8 %collective-permute-start.8 = (bf16[208,640]{1,0:T(8,128)(2,1)S(1)}, bf16[208,640]{1,0:T(8,128)(2,1)S(1)}, u32[]{:S(2)}, u32[]{:S(2)}) collective-permute-start(bf16[208,640]{1,0:T(8,128)(2,1)S(1)} %pick_selected.1.x0), channel_id=1, source_target_pairs={{0,6},{1,7},{2,0},{3,1},{4,2},{5,3},{6,4},{7,5},{8,14},{9,15},{10,... | collective-permute-start | bytes 798728 | tf_op jit(solution)/shard_map/ppermute | solution.py:430
  50.5 7.8 %collective-permute-done.8.x3 = bf16[208,640]{1,0:T(8,128)(2,1)S(1)} collective-permute-done((bf16[208,640]{1,0:T(8,128)(2,1)S(1)}, bf16[208,640]{1,0:T(8,128)(2,1)S(1)}, u32[]{:S(2)}, u32[]{:S(2)}) %collective-permute-start.8) | collective-permute-done | bytes 266272 | tf_op jit(solution)/shard_map/ppermute | solution.py:430
  58.4 3.7 %collective-permute-done.6.x1 = bf16[208,640]{1,0:T(8,128)(2,1)S(1)} collective-permute-done((bf16[208,640]{1,0:T(8,128)(2,1)S(1)}, bf16[208,640]{1,0:T(8,128)(2,1)S(1)}, u32[]{:S(2)}, u32[]{:S(2)}) %collective-permute-start.6) | collective-permute-done | bytes 266272 | tf_op jit(solution)/shard_map/ppermute | solution.py:430
  64.3 9.4 %scores.1 = (bf16[2176,640]{1,0:T(8,128)(2,1)S(1)}, bf16[4,2176,256]{2,1,0:T(8,128)(2,1)S(1)}, bf16[4,2176,256]{2,1,0:T(8,128)(2,1)S(1)}) custom-call(s32[2]{0:T(128)S(1)} %pad_add_fusion.me_ref, f32[16,128]{1,0:T(8,128)S(1)} %select_bitcast_fusion.far_ref, s32[1,128]{1,0:T(1,128)S(1)} %bitcast.13, bf16[208,640]{1,0:T(8,128)(2,1)S(1)} %pick_selected.1.x0, ...), custom_call_target="tpu_custom_call" | custom-call | flops 5133828096 | bytes 16000000 | tf_op jit(solution)/shard_map/scores/pallas_call | solution.py:273
  73.8 1.6 %dkv_chunk2.1 = (f32[272,640]{1,0:T(8,128)S(1)}, bf16[272,640]{1,0:T(8,128)(2,1)S(1)}) custom-call(bf16[4,2176,256]{2,1,0:T(8,128)(2,1)S(1)} %get-tuple-element.87.p_ref, bf16[4,2176,256]{2,1,0:T(8,128)(2,1)S(1)} %get-tuple-element.93.ds_ref, bf16[1024,640]{1,0:T(8,128)(2,1)S(1)} %get-tuple-element.70.q_ref, bf16[1024,512]{1,0:T(8,128)(2,1)S(1)} %get-tuple-element.71.g_ref), custom_call_target="tpu_custom_call" | custom-call | flops 1283457024 | bytes 5000000 | tf_op jit(solution)/shard_map/dkv_chunk2/pallas_call | solution.py:306
  75.6 1.6 %dkv_chunk1.1 = (f32[272,640]{1,0:T(8,128)S(1)}, bf16[272,640]{1,0:T(8,128)(2,1)S(1)}) custom-call(bf16[4,2176,256]{2,1,0:T(8,128)(2,1)S(1)} %get-tuple-element.87.p_ref, bf16[4,2176,256]{2,1,0:T(8,128)(2,1)S(1)} %get-tuple-element.93.ds_ref, bf16[1024,640]{1,0:T(8,128)(2,1)S(1)} %get-tuple-element.70.q_ref, bf16[1024,512]{1,0:T(8,128)(2,1)S(1)} %get-tuple-element.71.g_ref), custom_call_target="tpu_custom_call" | custom-call | flops 1283457024 | bytes 5000000 | tf_op jit(solution)/shard_map/dkv_chunk1/pallas_call | solution.py:306
  78.9 1.6 %dkv_chunk3.1 = (f32[272,640]{1,0:T(8,128)S(1)}, bf16[272,640]{1,0:T(8,128)(2,1)S(1)}) custom-call(bf16[4,2176,256]{2,1,0:T(8,128)(2,1)S(1)} %get-tuple-element.87.p_ref, bf16[4,2176,256]{2,1,0:T(8,128)(2,1)S(1)} %get-tuple-element.93.ds_ref, bf16[1024,640]{1,0:T(8,128)(2,1)S(1)} %get-tuple-element.70.q_ref, bf16[1024,512]{1,0:T(8,128)(2,1)S(1)} %get-tuple-element.71.g_ref), custom_call_target="tpu_custom_call" | custom-call | flops 1283457024 | bytes 5000000 | tf_op jit(solution)/shard_map/dkv_chunk3/pallas_call | solution.py:306
  80.7 1.3 %collective-permute-start.17 = (bf16[272,640]{1,0:T(8,128)(2,1)S(1)}, bf16[272,640]{1,0:T(8,128)(2,1)S(1)}, u32[]{:S(2)}, u32[]{:S(2)}) collective-permute-start(bf16[272,640]{1,0:T(8,128)(2,1)S(1)} %add_convert_fusion.1), channel_id=1, source_target_pairs={{0,6},{1,7},{2,0},{3,1},{4,2},{5,3},{6,4},{7,5},{8,14},{9,15},{10,... | collective-permute-start | bytes 1044488 | tf_op jit(solution)/shard_map/ppermute | solution.py:430
  82.0 1.6 %dkv_chunk0.1 = (f32[272,640]{1,0:T(8,128)S(1)}, bf16[272,640]{1,0:T(8,128)(2,1)S(1)}) custom-call(bf16[4,2176,256]{2,1,0:T(8,128)(2,1)S(1)} %get-tuple-element.87.p_ref, bf16[4,2176,256]{2,1,0:T(8,128)(2,1)S(1)} %get-tuple-element.93.ds_ref, bf16[1024,640]{1,0:T(8,128)(2,1)S(1)} %get-tuple-element.70.q_ref, bf16[1024,512]{1,0:T(8,128)(2,1)S(1)} %get-tuple-element.71.g_ref), custom_call_target="tpu_custom_call" | custom-call | flops 1283457024 | bytes 5000000 | tf_op jit(solution)/shard_map/dkv_chunk0/pallas_call | solution.py:306
  85.0 5.3 %dq.1 = (bf16[128,4096]{1,0:T(8,128)(2,1)}, bf16[128,512]{1,0:T(8,128)(2,1)}) custom-call(bf16[4,2176,256]{2,1,0:T(8,128)(2,1)S(1)} %get-tuple-element.93.ds_ref, bf16[2176,640]{1,0:T(8,128)(2,1)S(1)} %get-tuple-element.94.k_ref), custom_call_target="tpu_custom_call" | custom-call | flops 2852126720 | bytes 8000000 | tf_op jit(solution)/shard_map/dq/pallas_call | solution.py:332
  90.6 4.6 %collective-permute-done.17.r1_ref = bf16[272,640]{1,0:T(8,128)(2,1)S(1)} collective-permute-done((bf16[272,640]{1,0:T(8,128)(2,1)S(1)}, bf16[272,640]{1,0:T(8,128)(2,1)S(1)}, u32[]{:S(2)}, u32[]{:S(2)}) %collective-permute-start.17) | collective-permute-done | bytes 348192 | tf_op jit(solution)/shard_map/ppermute | solution.py:430
  95.3 2.0 %collective-permute-done.19.r3_ref = bf16[272,640]{1,0:T(8,128)(2,1)S(1)} collective-permute-done((bf16[272,640]{1,0:T(8,128)(2,1)S(1)}, bf16[272,640]{1,0:T(8,128)(2,1)S(1)}, u32[]{:S(2)}, u32[]{:S(2)}) %collective-permute-start.19) | collective-permute-done | bytes 348192 | tf_op jit(solution)/shard_map/ppermute | solution.py:430
  98.2 24.3 %all_to_all.22 = bf16[32,16,640]{2,1,0:T(8,128)(2,1)S(1)} all-to-all(bf16[32,16,640]{2,1,0:T(8,128)(2,1)S(1)} %bitcast.12), channel_id=1, replica_groups=mesh['ctx'=32,'head'=8] {'ctx'}, dimensions={0} | all-to-all | bytes 1310720 | tf_op jit(solution)/shard_map/all_to_all | solution.py:495
  (65 shorter events, 19.1 us)
Async XLA Ops:
  0.6 48.6 %copy-start.3 = (bf16[4,64,128]{2,1,0:T(8,128)(2,1)S(1)}, bf16[4,64,128]{2,1,0:T(8,128)(2,1)}, u32[]{:S(2)}) copy-start(bf16[4,64,128]{2,1,0:T(8,128)(2,1)} %rope_hbm) | copy-start | bytes 196612
  0.7 63.7 %copy-start.5 = (s32[128]{0:T(128)S(1)}, s32[128]{0:T(128)}, u32[]{:S(2)}) copy-start(s32[128]{0:T(128)} %param.13) | copy-start | bytes 1540
  2.8 28.8 %all-to-all-start = ((bf16[8,64,640]{2,1,0:T(8,128)(2,1)}), bf16[8,64,640]{2,1,0:T(8,128)(2,1)S(1)}, u32[]{:S(2)}, u32[]{:S(2)}) async-start(bf16[8,64,640]{2,1,0:T(8,128)(2,1)} %bitcast.14), calls=%async_computation | async-start | bytes 1310720 | tf_op jit(solution)/shard_map/all_to_all | solution.py:445
  12.8 49.8 %copy-start.6 = (s32[128,16]{0,1:T(8,128)S(1)}, s32[128,16]{0,1:T(8,128)}, u32[]{:S(2)}) copy-start(s32[128,16]{0,1:T(8,128)} %param.12) | copy-start | bytes 24580
  14.1 8.5 %collective-permute-start.2 = (s32[32]{0:T(128)S(1)}, s32[32]{0:T(128)S(1)}, u32[]{:S(2)}, u32[]{:S(2)}) collective-permute-start(s32[32]{0:T(128)S(1)} %select_reduce_fusion.refs_0_.want_ref), channel_id=1, source_target_pairs={{0,8},{8,16},{16,24},{24,0},{32,40},{40,48},{48,56},{56,32},{64,72... | collective-permute-start | bytes 392 | tf_op jit(solution)/shard_map/ppermute | solution.py:424
  15.8 6.9 %collective-permute-start.1 = (s32[32]{0:T(128)S(1)}, s32[32]{0:T(128)S(1)}, u32[]{:S(2)}, u32[]{:S(2)}) collective-permute-start(s32[32]{0:T(128)S(1)} %select_reduce_fusion.refs_0_.want_ref), channel_id=1, source_target_pairs={{0,16},{8,24},{16,0},{24,8},{32,48},{40,56},{48,32},{56,40},{64,80... | collective-permute-start | bytes 392 | tf_op jit(solution)/shard_map/ppermute | solution.py:424
  16.7 5.9 %collective-permute-start = (s32[32]{0:T(128)S(1)}, s32[32]{0:T(128)S(1)}, u32[]{:S(2)}, u32[]{:S(2)}) collective-permute-start(s32[32]{0:T(128)S(1)} %select_reduce_fusion.refs_0_.want_ref), channel_id=1, source_target_pairs={{0,24},{8,0},{16,8},{24,16},{32,56},{40,32},{48,40},{56,48},{64,88... | collective-permute-start | bytes 392 | tf_op jit(solution)/shard_map/ppermute | solution.py:424
  32.2 7.0 %collective-permute-start.3 = (bf16[128,640]{1,0:T(8,128)(2,1)S(1)}, bf16[128,640]{1,0:T(8,128)(2,1)S(1)}, u32[]{:S(2)}, u32[]{:S(2)}) collective-permute-start(bf16[128,640]{1,0:T(8,128)(2,1)S(1)} %get-tuple-element.58), channel_id=1, source_target_pairs={{0,8},{8,16},{16,24},{24,0},{32,40},{40,48},{48,56},{56,32},{64,72... | collective-permute-start | bytes 491528 | tf_op jit(solution)/shard_map/ppermute | solution.py:424
  33.9 8.6 %collective-permute-start.4 = (bf16[128,640]{1,0:T(8,128)(2,1)S(1)}, bf16[128,640]{1,0:T(8,128)(2,1)S(1)}, u32[]{:S(2)}, u32[]{:S(2)}) collective-permute-start(bf16[128,640]{1,0:T(8,128)(2,1)S(1)} %get-tuple-element.59), channel_id=1, source_target_pairs={{0,16},{8,24},{16,0},{24,8},{32,48},{40,56},{48,32},{56,40},{64,80... | collective-permute-start | bytes 491528 | tf_op jit(solution)/shard_map/ppermute | solution.py:424
  34.8 9.2 %collective-permute-start.5 = (bf16[128,640]{1,0:T(8,128)(2,1)S(1)}, bf16[128,640]{1,0:T(8,128)(2,1)S(1)}, u32[]{:S(2)}, u32[]{:S(2)}) collective-permute-start(bf16[128,640]{1,0:T(8,128)(2,1)S(1)} %get-tuple-element.60), channel_id=1, source_target_pairs={{0,24},{8,0},{16,8},{24,16},{32,56},{40,32},{48,40},{56,48},{64,88... | collective-permute-start | bytes 491528 | tf_op jit(solution)/shard_map/ppermute | solution.py:424
  44.7 13.7 %collective-permute-start.8 = (bf16[208,640]{1,0:T(8,128)(2,1)S(1)}, bf16[208,640]{1,0:T(8,128)(2,1)S(1)}, u32[]{:S(2)}, u32[]{:S(2)}) collective-permute-start(bf16[208,640]{1,0:T(8,128)(2,1)S(1)} %pick_selected.1.x0), channel_id=1, source_target_pairs={{0,6},{1,7},{2,0},{3,1},{4,2},{5,3},{6,4},{7,5},{8,14},{9,15},{10,... | collective-permute-start | bytes 798728 | tf_op jit(solution)/shard_map/ppermute | solution.py:430
  47.5 10.9 %collective-permute-start.7 = (bf16[208,640]{1,0:T(8,128)(2,1)S(1)}, bf16[208,640]{1,0:T(8,128)(2,1)S(1)}, u32[]{:S(2)}, u32[]{:S(2)}) collective-permute-start(bf16[208,640]{1,0:T(8,128)(2,1)S(1)} %pick_selected.1.x0), channel_id=1, source_target_pairs={{0,4},{1,5},{2,6},{3,7},{4,0},{5,1},{6,2},{7,3},{8,12},{9,13},{10,... | collective-permute-start | bytes 798728 | tf_op jit(solution)/shard_map/ppermute | solution.py:430
  48.3 13.7 %collective-permute-start.6 = (bf16[208,640]{1,0:T(8,128)(2,1)S(1)}, bf16[208,640]{1,0:T(8,128)(2,1)S(1)}, u32[]{:S(2)}, u32[]{:S(2)}) collective-permute-start(bf16[208,640]{1,0:T(8,128)(2,1)S(1)} %pick_selected.1.x0), channel_id=1, source_target_pairs={{0,2},{1,3},{2,4},{3,5},{4,6},{5,7},{6,0},{7,1},{8,10},{9,11},{10,... | collective-permute-start | bytes 798728 | tf_op jit(solution)/shard_map/ppermute | solution.py:430
  49.2 13.5 %collective-permute-start.9 = (bf16[208,640]{1,0:T(8,128)(2,1)S(1)}, bf16[208,640]{1,0:T(8,128)(2,1)S(1)}, u32[]{:S(2)}, u32[]{:S(2)}) collective-permute-start(bf16[208,640]{1,0:T(8,128)(2,1)S(1)} %pick_selected.1.x0), channel_id=1, source_target_pairs={{0,1},{1,0},{2,3},{3,2},{4,5},{5,4},{6,7},{7,6},{8,9},{9,8},{10,11... | collective-permute-start | bytes 798728 | tf_op jit(solution)/shard_map/ppermute | solution.py:434
  62.0 1.5 %collective-permute-start.10 = (bf16[208,640]{1,0:T(8,128)(2,1)S(1)}, bf16[208,640]{1,0:T(8,128)(2,1)S(1)}, u32[]{:S(2)}, u32[]{:S(2)}) collective-permute-start(bf16[208,640]{1,0:T(8,128)(2,1)S(1)} %collective-permute-done.6.x1), channel_id=1, source_target_pairs={{0,1},{1,0},{2,3},{3,2},{4,5},{5,4},{6,7},{7,6},{8,9},{9,8},{10,11... | collective-permute-start | bytes 798728 | tf_op jit(solution)/shard_map/ppermute | solution.py:434
  62.1 1.9 %collective-permute-start.11 = (bf16[208,640]{1,0:T(8,128)(2,1)S(1)}, bf16[208,640]{1,0:T(8,128)(2,1)S(1)}, u32[]{:S(2)}, u32[]{:S(2)}) collective-permute-start(bf16[208,640]{1,0:T(8,128)(2,1)S(1)} %collective-permute-done.7.x2), channel_id=1, source_target_pairs={{0,1},{1,0},{2,3},{3,2},{4,5},{5,4},{6,7},{7,6},{8,9},{9,8},{10,11... | collective-permute-start | bytes 798728 | tf_op jit(solution)/shard_map/ppermute | solution.py:434
  62.5 1.8 %collective-permute-start.12 = (bf16[208,640]{1,0:T(8,128)(2,1)S(1)}, bf16[208,640]{1,0:T(8,128)(2,1)S(1)}, u32[]{:S(2)}, u32[]{:S(2)}) collective-permute-start(bf16[208,640]{1,0:T(8,128)(2,1)S(1)} %collective-permute-done.8.x3), channel_id=1, source_target_pairs={{0,1},{1,0},{2,3},{3,2},{4,5},{5,4},{6,7},{7,6},{8,9},{9,8},{10,11... | collective-permute-start | bytes 798728 | tf_op jit(solution)/shard_map/ppermute | solution.py:434
  75.4 2.3 %collective-permute-start.13 = (bf16[272,640]{1,0:T(8,128)(2,1)S(1)}, bf16[272,640]{1,0:T(8,128)(2,1)S(1)}, u32[]{:S(2)}, u32[]{:S(2)}) collective-permute-start(bf16[272,640]{1,0:T(8,128)(2,1)S(1)} %get-tuple-element.74), channel_id=1, source_target_pairs={{0,1},{1,0},{2,3},{3,2},{4,5},{5,4},{6,7},{7,6},{8,9},{9,8},{10,11... | collective-permute-start | bytes 1044488 | tf_op jit(solution)/shard_map/ppermute | solution.py:434
  77.3 3.4 %collective-permute-start.14 = (bf16[272,640]{1,0:T(8,128)(2,1)S(1)}, bf16[272,640]{1,0:T(8,128)(2,1)S(1)}, u32[]{:S(2)}, u32[]{:S(2)}) collective-permute-start(bf16[272,640]{1,0:T(8,128)(2,1)S(1)} %get-tuple-element.77), channel_id=1, source_target_pairs={{0,1},{1,0},{2,3},{3,2},{4,5},{5,4},{6,7},{7,6},{8,9},{9,8},{10,11... | collective-permute-start | bytes 1044488 | tf_op jit(solution)/shard_map/ppermute | solution.py:434
  77.8 12.8 %collective-permute-start.18 = (bf16[272,640]{1,0:T(8,128)(2,1)S(1)}, bf16[272,640]{1,0:T(8,128)(2,1)S(1)}, u32[]{:S(2)}, u32[]{:S(2)}) collective-permute-start(bf16[272,640]{1,0:T(8,128)(2,1)S(1)} %add_convert_fusion.2), channel_id=1, source_target_pairs={{0,4},{1,5},{2,6},{3,7},{4,0},{5,1},{6,2},{7,3},{8,12},{9,13},{10,... | collective-permute-start | bytes 1044488 | tf_op jit(solution)/shard_map/ppermute | solution.py:430
  80.5 3.4 %collective-permute-start.15 = (bf16[272,640]{1,0:T(8,128)(2,1)S(1)}, bf16[272,640]{1,0:T(8,128)(2,1)S(1)}, u32[]{:S(2)}, u32[]{:S(2)}) collective-permute-start(bf16[272,640]{1,0:T(8,128)(2,1)S(1)} %get-tuple-element.83), channel_id=1, source_target_pairs={{0,1},{1,0},{2,3},{3,2},{4,5},{5,4},{6,7},{7,6},{8,9},{9,8},{10,11... | collective-permute-start | bytes 1044488 | tf_op jit(solution)/shard_map/ppermute | solution.py:434
  80.7 14.5 %collective-permute-start.17 = (bf16[272,640]{1,0:T(8,128)(2,1)S(1)}, bf16[272,640]{1,0:T(8,128)(2,1)S(1)}, u32[]{:S(2)}, u32[]{:S(2)}) collective-permute-start(bf16[272,640]{1,0:T(8,128)(2,1)S(1)} %add_convert_fusion.1), channel_id=1, source_target_pairs={{0,6},{1,7},{2,0},{3,1},{4,2},{5,3},{6,4},{7,5},{8,14},{9,15},{10,... | collective-permute-start | bytes 1044488 | tf_op jit(solution)/shard_map/ppermute | solution.py:430
  83.6 11.6 %collective-permute-start.16 = (bf16[272,640]{1,0:T(8,128)(2,1)S(1)}, bf16[272,640]{1,0:T(8,128)(2,1)S(1)}, u32[]{:S(2)}, u32[]{:S(2)}) collective-permute-start(bf16[272,640]{1,0:T(8,128)(2,1)S(1)} %get-tuple-element.90), channel_id=1, source_target_pairs={{0,1},{1,0},{2,3},{3,2},{4,5},{5,4},{6,7},{7,6},{8,9},{9,8},{10,11... | collective-permute-start | bytes 1044488 | tf_op jit(solution)/shard_map/ppermute | solution.py:434
  84.0 13.3 %collective-permute-start.19 = (bf16[272,640]{1,0:T(8,128)(2,1)S(1)}, bf16[272,640]{1,0:T(8,128)(2,1)S(1)}, u32[]{:S(2)}, u32[]{:S(2)}) collective-permute-start(bf16[272,640]{1,0:T(8,128)(2,1)S(1)} %add_convert_fusion), channel_id=1, source_target_pairs={{0,2},{1,3},{2,4},{3,5},{4,6},{5,7},{6,0},{7,1},{8,10},{9,11},{10,... | collective-permute-start | bytes 1044488 | tf_op jit(solution)/shard_map/ppermute | solution.py:430
  (4 other events, 194.3 us)
where the time goes:
time: 124 us
  waiting for transfers between devices  35.7 us (29%)
  Pallas kernels  28.1 us (23%)
  starting transfers between devices  27.9 us (22%)
  blocking collectives  24.3 us (20%)
  other arithmetic  5.13 us (4%)
  local copies, waits for them, and re-layouts  1.76 us (1%)
    all_to_all x1, blocking collectives, local(): back = lax.all_to_all(slots, 'ctx', split_axis=0, concat_axis=0, tiled=True)  24.3 us
    ppermute x6, waiting for transfers between devices, step_x(): lax.ppermute(a, 'head', [(i, (i + 2 * d) % (2 * NX)) for i in range(2 * N...  18.4 us
    ppermute x6, starting transfers between devices, step_y(): lax.ppermute(a, 'ctx', [(z * NY + y, z * NY + (y + d) % NY) for z in rang...  10 us
    pallas_call x1, Pallas kernels, scores_call(): pl.pallas_call(scores_body, in_specs=[pl.BlockSpec(memory_space=pltpu.SME...  9.45 us
    all_to_all x1, waiting for transfers between devices, local(): lax.all_to_all(shard, 'ctx', 0, 0, tiled=True, axis_index_groups=columns)  8.9 us
    all_to_all x1, starting transfers between devices, local(): lax.all_to_all(shard, 'ctx', 0, 0, tiled=True, axis_index_groups=columns)  8.48 us
    ppermute x6, starting transfers between devices, step_x(): lax.ppermute(a, 'head', [(i, (i + 2 * d) % (2 * NX)) for i in range(2 * N...  7.81 us
    ppermute x6, waiting for transfers between devices, step_y(): lax.ppermute(a, 'ctx', [(z * NY + y, z * NY + (y + d) % NY) for z in rang...  6.8 us
  transfers between devices with their start and end apart: 21, of which 12 were waited for; matrix products, arithmetic and copies ran while one was open for 6% of the time, Pallas kernels for 9%

commit v1 on v0

--- a/solution.py
+++ b/solution.py
@@ -28,6 +28,15 @@
 NCH = ROWS // CH
 SPAN = OWN * SHARE
 SLOTS = 32
+TILES = LAT // 128
+BLOCK_ROWS = TILES * SHARE
+SHARD_ROWS = OWN * BLOCK_ROWS + OWN // 2 * SHARE
+COL_LAT = 8 * BLOCK_ROWS
+COL_ROWS = COL_LAT + 4 * SHARE
+FAR_LAT = REMOTE * BLOCK_ROWS
+FAR_PACKED = FAR_LAT + (REMOTE + 1) // 2 * SHARE
+GRAD_LAT = (REMOTE + OWN) * BLOCK_ROWS
+GRAD_ROWS = GRAD_LAT + (REMOTE + OWN + 1) // 2 * SHARE
 NZ, NY, NX = 8, 4, 4
 
 
@@ -57,6 +66,21 @@
 
 def tn_dot(a, b):
     return lax.dot_general(a, b, (((0,), (0,)), ((), ())), preferred_element_type=F32)
+
+
+def left_lanes(wide):
+    lane = lax.broadcasted_iota(jnp.int32, wide.shape, 1)
+    return jnp.where(lane < 64, wide, 0.0)
+
+
+def pair_tile(even, odd):
+    lane = lax.broadcasted_iota(jnp.int32, even.shape, 1)
+    return jnp.where(lane < 64, even, pltpu.roll(odd, 64, 1))
+
+
+def half_tile(tile, odd):
+    wide = tile.astype(F32)
+    return jnp.where(odd == 1, pltpu.roll(wide, 64, 1), wide)
 
 
 def unpack_rope(packed, core):
@@ -64,10 +88,8 @@
     col = lax.broadcasted_iota(jnp.int32, (SHARE, SHARE), 1)
     pick = jnp.where(col == core * 8 + row // 2, 1.0, 0.0).astype(BF)
     wide = jnp.dot(pick, packed, preferred_element_type=F32)
-    lane = lax.broadcasted_iota(jnp.int32, (SHARE, 128), 1)
     odd = lax.broadcasted_iota(jnp.int32, (SHARE, 128), 0) % 2 == 1
-    both = jnp.where(odd, pltpu.roll(wide, 64, 1), wide)
-    return jnp.where(lane < 64, both, 0.0).astype(BF)
+    return left_lanes(jnp.where(odd, pltpu.roll(wide, 64, 1), wide))
 
 
 def pack_body(kv_ref, rope_ref, out_ref, lat, rope, sems):
@@ -82,12 +104,13 @@
         copy.start()
     for copy in copies:
         copy.wait()
-    for b in range(OWN):
-        thin_rows = unpack_rope(rope[b], head % 2)
-        for z in range(NZ):
-            rows = slice(z * SPAN + b * SHARE, z * SPAN + (b + 1) * SHARE)
-            out_ref[rows, :LAT] = lat[b]
-            out_ref[rows, LAT:] = thin_rows
+    tiles = [lat[b, :, t * 128:(t + 1) * 128] for b in range(OWN) for t in range(TILES)]
+    thin_rows = [unpack_rope(rope[b], head % 2) for b in range(OWN)]
+    tiles += [pair_tile(*thin_rows[b:b + 2]).astype(BF) for b in range(0, OWN, 2)]
+    for z in range(NZ):
+        for n, tile in enumerate(tiles):
+            at = z * SHARD_ROWS + n * SHARE
+            out_ref[at:at + SHARE, :] = tile
 
 
 def pack_call(kv, rope):
@@ -95,7 +118,7 @@
         pack_body,
         in_specs=[hbm_spec()] * 2,
         out_specs=vspec(),
-        out_shape=jax.ShapeDtypeStruct((NZ * SPAN, WIDE), BF),
+        out_shape=jax.ShapeDtypeStruct((NZ * SHARD_ROWS, 128), BF),
         scratch_shapes=[
             pltpu.VMEM((OWN, SHARE, LAT), BF),
             pltpu.VMEM((OWN, SHARE, 128), BF),
@@ -139,7 +162,7 @@
         for b in range(OWN):
             own_out[g, b * SHARE:(b + 1) * SHARE, LAT:] = unpack_rope(
                 rope_ref[b, pl.ds(pl.multiple_of(chip * SHARE, SHARE), SHARE), :], core
-            )
+            ).astype(BF)
     copies[2].wait()
     for g in range(GROUPS):
         chip, core = share_of(me, g)
@@ -172,15 +195,27 @@
     )(kv, rope, q, qr, g)
 
 
+def rows_at(ref, at, count):
+    return ref[pl.ds(pl.multiple_of(at, SHARE), count), :]
+
+
 def pick_y_body(*refs):
     wants, shards, outs = refs[:NY], refs[NY], refs[NY + 1:]
     ctx = lax.axis_index("ctx")
-    for r in range(NZ):
-        z = (ctx // NY + NZ - r) % NZ
-        for dy in range(NY):
+    for dy in range(NY):
+        thin = []
+        for r in range(NZ):
+            z = (ctx // NY + NZ - r) % NZ
             w = jnp.maximum(wants[dy][z * NY + ctx % NY], 0)
-            at = pl.multiple_of((z * OWN + w) * SHARE, SHARE)
-            outs[dy][r * SHARE:(r + 1) * SHARE, :] = shards[pl.ds(at, SHARE), :]
+            base = z * SHARD_ROWS
+            outs[dy][r * BLOCK_ROWS:(r + 1) * BLOCK_ROWS, :] = rows_at(
+                shards, base + w * BLOCK_ROWS, BLOCK_ROWS
+            )
+            tile = rows_at(shards, base + OWN * BLOCK_ROWS + w // 2 * SHARE, SHARE)
+            thin.append(half_tile(tile, w % 2))
+        for r in range(0, NZ, 2):
+            at = COL_LAT + r // 2 * SHARE
+            outs[dy][at:at + SHARE, :] = pair_tile(thin[r], thin[r + 1]).astype(BF)
 
 
 def pick_y_call(wants, shards):
@@ -188,19 +223,26 @@
         pick_y_body,
         in_specs=[pl.BlockSpec(memory_space=pltpu.SMEM)] * NY + [vspec()],
         out_specs=[vspec()] * NY,
-        out_shape=[jax.ShapeDtypeStruct((NZ * SHARE, WIDE), BF)] * NY,
+        out_shape=[jax.ShapeDtypeStruct((COL_ROWS, 128), BF)] * NY,
         compiler_params=params(4),
         name="pick_for_y_peers",
     )(*wants, shards)
 
 
 def pick_x_body(src_ref, y0, y1, y2, y3, out_ref, stage):
-    span = NZ * SHARE
     for dy, ref in enumerate((y0, y1, y2, y3)):
-        stage[dy * span:(dy + 1) * span, :] = ref[...]
+        stage[dy * COL_ROWS:(dy + 1) * COL_ROWS, :] = ref[...]
+    thin = []
     for u in range(REMOTE):
-        at = pl.multiple_of(src_ref[u] * SHARE, SHARE)
-        out_ref[u * SHARE:(u + 1) * SHARE, :] = stage[pl.ds(at, SHARE), :]
+        base, r = src_ref[u] // NZ * COL_ROWS, src_ref[u] % NZ
+        out_ref[u * BLOCK_ROWS:(u + 1) * BLOCK_ROWS, :] = rows_at(
+            stage, base + r * BLOCK_ROWS, BLOCK_ROWS
+        )
+        thin.append(half_tile(rows_at(stage, base + COL_LAT + r // 2 * SHARE, SHARE), r % 2))
+    for u in range(0, REMOTE, 2):
+        at = FAR_LAT + u // 2 * SHARE
+        odd = thin[min(u + 1, REMOTE - 1)]
+        out_ref[at:at + SHARE, :] = pair_tile(thin[u], odd).astype(BF)
 
 
 def pick_x_call(src, cols):
@@ -208,8 +250,8 @@
         pick_x_body,
         in_specs=[pl.BlockSpec(memory_space=pltpu.SMEM)] + [vspec()] * NY,
         out_specs=vspec(),
-        out_shape=jax.ShapeDtypeStruct((FAR_ROWS, WIDE), BF),
-        scratch_shapes=[pltpu.VMEM((NY * NZ * SHARE, WIDE), BF)],
+        out_shape=jax.ShapeDtypeStruct((FAR_PACKED, 128), BF),
+        scratch_shapes=[pltpu.VMEM((NY * COL_ROWS, 128), BF)],
         compiler_params=params(4),
         name="pick_selected",
     )(src, *cols)
@@ -231,7 +273,13 @@
             key = step + (b * 128 + (chip * 2 + core) * SHARE)
             bias_scr[at:at + SHARE, :] = jnp.where(key <= pos, 0.0, NEG_FILL)
     for g, ref in enumerate((x0, c0, x1, c1, x2, c2, x3, c3)):
-        k_out[g * GROUP:g * GROUP + FAR_ROWS, :] = ref[...]
+        for u in range(REMOTE):
+            rows = slice(g * GROUP + u * SHARE, g * GROUP + (u + 1) * SHARE)
+            for t in range(TILES):
+                at = u * BLOCK_ROWS + t * SHARE
+                k_out[rows, t * 128:(t + 1) * 128] = ref[at:at + SHARE, :]
+            at = FAR_LAT + u // 2 * SHARE
+            k_out[rows, LAT:] = left_lanes(half_tile(ref[at:at + SHARE, :], u % 2)).astype(BF)
         k_out[g * GROUP + FAR_ROWS:(g + 1) * GROUP, :] = own[g]
 
     def chunk(c, carry):
@@ -297,8 +345,17 @@
         p = jnp.concatenate([p_ref[c, rows, :] for c in range(NCH)], axis=1)
         a = jnp.dot(ds, q_ref[...], preferred_element_type=F32)
         b = jnp.dot(p, g_ref[...], preferred_element_type=F32)
-        out[:, :LAT] = (a[:, :LAT] + b).astype(out.dtype)
-        out[:, LAT:] = a[:, LAT:].astype(out.dtype)
+        lat, thin = a[:, :LAT] + b, a[:, LAT:]
+        for u in range(REMOTE + OWN):
+            mine = slice(u * SHARE, (u + 1) * SHARE)
+            for t in range(TILES):
+                at = u * BLOCK_ROWS + t * SHARE
+                out[at:at + SHARE, :] = lat[mine, t * 128:(t + 1) * 128].astype(out.dtype)
+        for u in range(0, REMOTE + OWN, 2):
+            at = GRAD_LAT + u // 2 * SHARE
+            odd = min(u + 1, REMOTE + OWN - 1)
+            pair = pair_tile(thin[u * SHARE:(u + 1) * SHARE], thin[odd * SHARE:(odd + 1) * SHARE])
+            out[at:at + SHARE, :] = pair.astype(out.dtype)
 
 
 def dkv_call(dx, p, ds, q, g):
@@ -308,10 +365,10 @@
         grid=(1,),
         in_specs=[part, part, pl.BlockSpec((ROWS, WIDE), lambda i: (0, 0)),
                   pl.BlockSpec((ROWS, LAT), lambda i: (0, 0))],
-        out_specs=[pl.BlockSpec((GROUP, WIDE), lambda i: (0, 0))] * 2,
+        out_specs=[pl.BlockSpec((GRAD_ROWS, 128), lambda i: (0, 0))] * 2,
         out_shape=[
-            jax.ShapeDtypeStruct((GROUP, WIDE), F32),
-            jax.ShapeDtypeStruct((GROUP, WIDE), BF),
+            jax.ShapeDtypeStruct((GRAD_ROWS, 128), F32),
+            jax.ShapeDtypeStruct((GRAD_ROWS, 128), BF),
         ],
         compiler_params=params(16),
         cost_estimate=cost(2 * CHIP * ROWS * 1152, 5_000_000),
@@ -355,16 +412,25 @@
     total = keep_ref[...] + swap_ref[...].astype(F32)
     for ref in (r1_ref, r2_ref, r3_ref):
         total = total + ref[...].astype(F32)
-    own_out[...] = total[FAR_ROWS:, :]
-    far[...] = total[:FAR_ROWS, :]
+    far[...] = total
+    for b in range(OWN):
+        u, rows = REMOTE + b, slice(b * SHARE, (b + 1) * SHARE)
+        for t in range(TILES):
+            at = u * BLOCK_ROWS + t * SHARE
+            own_out[rows, t * 128:(t + 1) * 128] = far[at:at + SHARE, :]
+        at = GRAD_LAT + u // 2 * SHARE
+        own_out[rows, LAT:] = left_lanes(half_tile(far[at:at + SHARE, :], u % 2))
     lane = lax.broadcasted_iota(jnp.int32, (SHARE, 128), 1)
     for c in range(SLOTS):
         rows = slice(c * SHARE, (c + 1) * SHARE)
         w = want_ref[c]
         flag = jnp.where(w >= 0, 64 + w, 128)
-        piece = far[pl.ds(pl.multiple_of(at_ref[c] * SHARE, SHARE), SHARE), :]
-        slot_out[rows, :LAT] = piece[:, :LAT].astype(BF)
-        slot_out[rows, LAT:] = jnp.where(lane == flag, 1.0, piece[:, LAT:]).astype(BF)
+        u = at_ref[c]
+        for t in range(TILES):
+            tile = rows_at(far, u * BLOCK_ROWS + t * SHARE, SHARE)
+            slot_out[rows, t * 128:(t + 1) * 128] = tile.astype(BF)
+        thin = left_lanes(half_tile(rows_at(far, GRAD_LAT + u // 2 * SHARE, SHARE), u % 2))
+        slot_out[rows, LAT:] = jnp.where(lane == flag, 1.0, thin).astype(BF)
 
 
 def slots_call(at, want, keep, swap, r1, r2, r3):
@@ -377,7 +443,7 @@
             jax.ShapeDtypeStruct((SLOTS * SHARE, WIDE), BF),
             jax.ShapeDtypeStruct((SPAN, WIDE), F32),
         ],
-        scratch_shapes=[pltpu.VMEM((FAR_ROWS, WIDE), F32)],
+        scratch_shapes=[pltpu.VMEM((GRAD_ROWS, 128), F32)],
         compiler_params=params(8),
         name="fill_slots",
     )(at, want, keep, swap, r1, r2, r3)

time: 124 us -> 120 us (0.968)
  other arithmetic: 5.13 us -> 1.51 us
  waiting for transfers between devices: 35.7 us -> 33.7 us
    ppermute x6, waiting for transfers between devices: 18.4 us -> 14.3 us  [step_x(): lax.ppermute(a, 'head', [(i, (i + 2 * d) % (2 * NX)) for i in range(2 * N...]
    unnamed x14, local copies, waits for them, and re-layouts: 0.03 us -> 1.76 us
    all_to_all x1, waiting for transfers between devices: 8.9 us -> 10.6 us  [local(): lax.all_to_all(shard, 'ctx', 0, 0, tiled=True, axis_index_groups=columns)]
    another operation x1, other arithmetic: 1.61 us -> 0.17 us
  transfers between devices with their start and end apart: 21 -> 21, of which waited for: 12 -> 13; matrix products, arithmetic and copies ran while one was open for 6% -> 2% of each run, Pallas kernels for 9% -> 10%
where the time goes in v1:
time: 120 us
  waiting for transfers between devices  33.7 us (28%)
  Pallas kernels  28.7 us (24%)
  starting transfers between devices  27.9 us (23%)
  blocking collectives  24.1 us (20%)
  local copies, waits for them, and re-layouts  2.89 us (2%)
  other arithmetic  1.51 us (1%)
    all_to_all x1, blocking collectives, local(): back = lax.all_to_all(slots, 'ctx', split_axis=0, concat_axis=0, tiled=True)  24.1 us
    ppermute x6, waiting for transfers between devices, step_x(): lax.ppermute(a, 'head', [(i, (i + 2 * d) % (2 * NX)) for i in range(2 * N...  14.3 us
    all_to_all x1, waiting for transfers between devices, local(): lax.all_to_all(shard, 'ctx', 0, 0, tiled=True, axis_index_groups=columns)  10.6 us
    ppermute x6, starting transfers between devices, step_y(): lax.ppermute(a, 'ctx', [(z * NY + y, z * NY + (y + d) % NY) for z in rang...  10 us
    pallas_call x1, Pallas kernels, scores_call(): pl.pallas_call(scores_body, in_specs=[pl.BlockSpec(memory_space=pltpu.SME...  9.52 us
    all_to_all x1, starting transfers between devices, local(): lax.all_to_all(shard, 'ctx', 0, 0, tiled=True, axis_index_groups=columns)  8.48 us
    ppermute x6, starting transfers between devices, step_x(): lax.ppermute(a, 'head', [(i, (i + 2 * d) % (2 * NX)) for i in range(2 * N...  7.79 us
    ppermute x6, waiting for transfers between devices, step_y(): lax.ppermute(a, 'ctx', [(z * NY + y, z * NY + (y + d) % NY) for z in rang...  7.19 us
  transfers between devices with their start and end apart: 21, of which 13 were waited for; matrix products, arithmetic and copies ran while one was open for 2% of the time, Pallas kernels for 10%

profile of v1, /device:TPU:8, one launch (start us, length us, event | category | flops | bytes accessed | tf_op | source)
XLA Modules:
  0.0 119.5 jit_solution(7977679134460431750)
XLA Ops:
  0.7 2.1 %pack_share.1 = bf16[2304,128]{1,0:T(8,128)(2,1)} custom-call(bf16[4,128,512]{2,1,0:T(8,128)(2,1)} %kv_hbm, bf16[4,64,128]{2,1,0:T(8,128)(2,1)} %rope_hbm), custom_call_target="tpu_custom_call" | custom-call | tf_op jit(solution)/shard_map/pack_share/pallas_call | solution.py:117
  2.8 8.5 %all-to-all-start = ((bf16[8,288,128]{2,1,0:T(8,128)(2,1)}), bf16[8,288,128]{2,1,0:T(8,128)(2,1)S(1)}, u32[]{:S(2)}, u32[]{:S(2)}) async-start(bf16[8,288,128]{2,1,0:T(8,128)(2,1)} %bitcast.14), calls=%async_computation | async-start | bytes 1179648 | tf_op jit(solution)/shard_map/all_to_all | solution.py:511
  12.8 1.7 %collective-permute-start.2 = (s32[32]{0:T(128)S(1)}, s32[32]{0:T(128)S(1)}, u32[]{:S(2)}, u32[]{:S(2)}) collective-permute-start(s32[32]{0:T(128)S(1)} %select_reduce_fusion.refs_0_.want_ref), channel_id=1, source_target_pairs={{0,8},{8,16},{16,24},{24,0},{32,40},{40,48},{48,56},{56,32},{64,72... | collective-permute-start | bytes 392 | tf_op jit(solution)/shard_map/ppermute | solution.py:490
  15.4 2.4 %collective-permute-start = (s32[32]{0:T(128)S(1)}, s32[32]{0:T(128)S(1)}, u32[]{:S(2)}, u32[]{:S(2)}) collective-permute-start(s32[32]{0:T(128)S(1)} %select_reduce_fusion.refs_0_.want_ref), channel_id=1, source_target_pairs={{0,24},{8,0},{16,8},{24,16},{32,56},{40,32},{48,40},{56,48},{64,88... | collective-permute-start | bytes 392 | tf_op jit(solution)/shard_map/ppermute | solution.py:490
  19.5 10.6 %all-to-all-done = bf16[8,288,128]{2,1,0:T(8,128)(2,1)S(1)} async-done(((bf16[8,288,128]{2,1,0:T(8,128)(2,1)}), bf16[8,288,128]{2,1,0:T(8,128)(2,1)S(1)}, u32[]{:S(2)}, u32[]{:S(2)}) %all-to-all-start) | async-done | bytes 589856 | tf_op jit(solution)/shard_map/all_to_all | solution.py:511
  31.1 1.7 %collective-permute-start.3 = (bf16[576,128]{1,0:T(8,128)(2,1)S(1)}, bf16[576,128]{1,0:T(8,128)(2,1)S(1)}, u32[]{:S(2)}, u32[]{:S(2)}) collective-permute-start(bf16[576,128]{1,0:T(8,128)(2,1)S(1)} %get-tuple-element.58), channel_id=1, source_target_pairs={{0,8},{8,16},{16,24},{24,0},{32,40},{40,48},{48,56},{56,32},{64,72... | collective-permute-start | bytes 442376 | tf_op jit(solution)/shard_map/ppermute | solution.py:490
  33.7 2.4 %collective-permute-start.5 = (bf16[576,128]{1,0:T(8,128)(2,1)S(1)}, bf16[576,128]{1,0:T(8,128)(2,1)S(1)}, u32[]{:S(2)}, u32[]{:S(2)}) collective-permute-start(bf16[576,128]{1,0:T(8,128)(2,1)S(1)} %get-tuple-element.60), channel_id=1, source_target_pairs={{0,24},{8,0},{16,8},{24,16},{32,56},{40,32},{48,40},{56,48},{64,88... | collective-permute-start | bytes 442376 | tf_op jit(solution)/shard_map/ppermute | solution.py:490
  36.1 1.3 %collective-permute-done.3.y1 = bf16[576,128]{1,0:T(8,128)(2,1)S(1)} collective-permute-done((bf16[576,128]{1,0:T(8,128)(2,1)S(1)}, bf16[576,128]{1,0:T(8,128)(2,1)S(1)}, u32[]{:S(2)}, u32[]{:S(2)}) %collective-permute-start.3) | collective-permute-done | bytes 147488 | tf_op jit(solution)/shard_map/ppermute | solution.py:490
  37.4 3.6 %collective-permute-done.4.y2 = bf16[576,128]{1,0:T(8,128)(2,1)S(1)} collective-permute-done((bf16[576,128]{1,0:T(8,128)(2,1)S(1)}, bf16[576,128]{1,0:T(8,128)(2,1)S(1)}, u32[]{:S(2)}, u32[]{:S(2)}) %collective-permute-start.4) | collective-permute-done | bytes 147488 | tf_op jit(solution)/shard_map/ppermute | solution.py:490
  41.0 1.2 %collective-permute-done.5.y3 = bf16[576,128]{1,0:T(8,128)(2,1)S(1)} collective-permute-done((bf16[576,128]{1,0:T(8,128)(2,1)S(1)}, bf16[576,128]{1,0:T(8,128)(2,1)S(1)}, u32[]{:S(2)}, u32[]{:S(2)}) %collective-permute-start.5) | collective-permute-done | bytes 147488 | tf_op jit(solution)/shard_map/ppermute | solution.py:490
  43.0 2.8 %collective-permute-start.8 = (bf16[944,128]{1,0:T(8,128)(2,1)S(1)}, bf16[944,128]{1,0:T(8,128)(2,1)S(1)}, u32[]{:S(2)}, u32[]{:S(2)}) collective-permute-start(bf16[944,128]{1,0:T(8,128)(2,1)S(1)} %pick_selected.1.x0), channel_id=1, source_target_pairs={{0,6},{1,7},{2,0},{3,1},{4,2},{5,3},{6,4},{7,5},{8,14},{9,15},{10,... | collective-permute-start | bytes 725000 | tf_op jit(solution)/shard_map/ppermute | solution.py:496
  50.5 5.1 %collective-permute-done.8.x3 = bf16[944,128]{1,0:T(8,128)(2,1)S(1)} collective-permute-done((bf16[944,128]{1,0:T(8,128)(2,1)S(1)}, bf16[944,128]{1,0:T(8,128)(2,1)S(1)}, u32[]{:S(2)}, u32[]{:S(2)}) %collective-permute-start.8) | collective-permute-done | bytes 241696 | tf_op jit(solution)/shard_map/ppermute | solution.py:496
  56.2 3.1 %collective-permute-done.6.x1 = bf16[944,128]{1,0:T(8,128)(2,1)S(1)} collective-permute-done((bf16[944,128]{1,0:T(8,128)(2,1)S(1)}, bf16[944,128]{1,0:T(8,128)(2,1)S(1)}, u32[]{:S(2)}, u32[]{:S(2)}) %collective-permute-start.6) | collective-permute-done | bytes 241696 | tf_op jit(solution)/shard_map/ppermute | solution.py:496
  61.5 9.5 %scores.1 = (bf16[2176,640]{1,0:T(8,128)(2,1)S(1)}, bf16[4,2176,256]{2,1,0:T(8,128)(2,1)S(1)}, bf16[4,2176,256]{2,1,0:T(8,128)(2,1)S(1)}) custom-call(s32[2]{0:T(128)S(1)} %pad_add_fusion.me_ref, f32[16,128]{1,0:T(8,128)S(1)} %select_bitcast_fusion.far_ref, s32[1,128]{1,0:T(1,128)S(1)} %bitcast.13, bf16[944,128]{1,0:T(8,128)(2,1)S(1)} %pick_selected.1.x0, ...), custom_call_target="tpu_custom_call" | custom-call | flops 5133828096 | bytes 16000000 | tf_op jit(solution)/shard_map/scores/pallas_call | solution.py:321
  71.0 1.6 %dkv_chunk2.1 = (f32[1232,128]{1,0:T(8,128)S(1)}, bf16[1232,128]{1,0:T(8,128)(2,1)S(1)}) custom-call(bf16[4,2176,256]{2,1,0:T(8,128)(2,1)S(1)} %get-tuple-element.87.p_ref, bf16[4,2176,256]{2,1,0:T(8,128)(2,1)S(1)} %get-tuple-element.93.ds_ref, bf16[1024,640]{1,0:T(8,128)(2,1)S(1)} %get-tuple-element.70.q_ref, bf16[1024,512]{1,0:T(8,128)(2,1)S(1)} %get-tuple-element.71.g_ref), custom_call_target="tpu_custom_call" | custom-call | flops 1283457024 | bytes 5000000 | tf_op jit(solution)/shard_map/dkv_chunk2/pallas_call | solution.py:363
  72.9 1.6 %dkv_chunk1.1 = (f32[1232,128]{1,0:T(8,128)S(1)}, bf16[1232,128]{1,0:T(8,128)(2,1)S(1)}) custom-call(bf16[4,2176,256]{2,1,0:T(8,128)(2,1)S(1)} %get-tuple-element.87.p_ref, bf16[4,2176,256]{2,1,0:T(8,128)(2,1)S(1)} %get-tuple-element.93.ds_ref, bf16[1024,640]{1,0:T(8,128)(2,1)S(1)} %get-tuple-element.70.q_ref, bf16[1024,512]{1,0:T(8,128)(2,1)S(1)} %get-tuple-element.71.g_ref), custom_call_target="tpu_custom_call" | custom-call | flops 1283457024 | bytes 5000000 | tf_op jit(solution)/shard_map/dkv_chunk1/pallas_call | solution.py:363
  76.1 1.6 %dkv_chunk3.1 = (f32[1232,128]{1,0:T(8,128)S(1)}, bf16[1232,128]{1,0:T(8,128)(2,1)S(1)}) custom-call(bf16[4,2176,256]{2,1,0:T(8,128)(2,1)S(1)} %get-tuple-element.87.p_ref, bf16[4,2176,256]{2,1,0:T(8,128)(2,1)S(1)} %get-tuple-element.93.ds_ref, bf16[1024,640]{1,0:T(8,128)(2,1)S(1)} %get-tuple-element.70.q_ref, bf16[1024,512]{1,0:T(8,128)(2,1)S(1)} %get-tuple-element.71.g_ref), custom_call_target="tpu_custom_call" | custom-call | flops 1283457024 | bytes 5000000 | tf_op jit(solution)/shard_map/dkv_chunk3/pallas_call | solution.py:363
  77.9 1.3 %collective-permute-start.17 = (bf16[1232,128]{1,0:T(8,128)(2,1)S(1)}, bf16[1232,128]{1,0:T(8,128)(2,1)S(1)}, u32[]{:S(2)}, u32[]{:S(2)}) collective-permute-start(bf16[1232,128]{1,0:T(8,128)(2,1)S(1)} %add_convert_fusion.1), channel_id=1, source_target_pairs={{0,6},{1,7},{2,0},{3,1},{4,2},{5,3},{6,4},{7,5},{8,14},{9,15},{10,... | collective-permute-start | bytes 946184 | tf_op jit(solution)/shard_map/ppermute | solution.py:496
  79.2 1.6 %dkv_chunk0.1 = (f32[1232,128]{1,0:T(8,128)S(1)}, bf16[1232,128]{1,0:T(8,128)(2,1)S(1)}) custom-call(bf16[4,2176,256]{2,1,0:T(8,128)(2,1)S(1)} %get-tuple-element.87.p_ref, bf16[4,2176,256]{2,1,0:T(8,128)(2,1)S(1)} %get-tuple-element.93.ds_ref, bf16[1024,640]{1,0:T(8,128)(2,1)S(1)} %get-tuple-element.70.q_ref, bf16[1024,512]{1,0:T(8,128)(2,1)S(1)} %get-tuple-element.71.g_ref), custom_call_target="tpu_custom_call" | custom-call | flops 1283457024 | bytes 5000000 | tf_op jit(solution)/shard_map/dkv_chunk0/pallas_call | solution.py:363
  82.2 5.3 %dq.1 = (bf16[128,4096]{1,0:T(8,128)(2,1)}, bf16[128,512]{1,0:T(8,128)(2,1)}) custom-call(bf16[4,2176,256]{2,1,0:T(8,128)(2,1)S(1)} %get-tuple-element.93.ds_ref, bf16[2176,640]{1,0:T(8,128)(2,1)S(1)} %get-tuple-element.94.k_ref), custom_call_target="tpu_custom_call" | custom-call | flops 2852126720 | bytes 8000000 | tf_op jit(solution)/shard_map/dq/pallas_call | solution.py:389
  87.5 3.5 %collective-permute-done.17.r1_ref = bf16[1232,128]{1,0:T(8,128)(2,1)S(1)} collective-permute-done((bf16[1232,128]{1,0:T(8,128)(2,1)S(1)}, bf16[1232,128]{1,0:T(8,128)(2,1)S(1)}, u32[]{:S(2)}, u32[]{:S(2)}) %collective-permute-start.17) | collective-permute-done | bytes 315424 | tf_op jit(solution)/shard_map/ppermute | solution.py:496
  91.1 2.0 %collective-permute-done.19.r3_ref = bf16[1232,128]{1,0:T(8,128)(2,1)S(1)} collective-permute-done((bf16[1232,128]{1,0:T(8,128)(2,1)S(1)}, bf16[1232,128]{1,0:T(8,128)(2,1)S(1)}, u32[]{:S(2)}, u32[]{:S(2)}) %collective-permute-start.19) | collective-permute-done | bytes 315424 | tf_op jit(solution)/shard_map/ppermute | solution.py:496
  94.2 24.1 %all_to_all.22 = bf16[32,16,640]{2,1,0:T(8,128)(2,1)S(1)} all-to-all(bf16[32,16,640]{2,1,0:T(8,128)(2,1)S(1)} %bitcast.12), channel_id=1, replica_groups=mesh['ctx'=32,'head'=8] {'ctx'}, dimensions={0} | all-to-all | bytes 1310720 | tf_op jit(solution)/shard_map/all_to_all | solution.py:561
  118.3 1.3 %finish.1 = (f32[4,16,512]{2,1,0:T(8,128)}, f32[4,8,128]{2,1,0:T(8,128)}) custom-call(f32[64,640]{1,0:T(8,128)S(1)} %get-tuple-element.100.own_ref, bf16[512,640]{1,0:T(8,128)(2,1)S(1)} %bitcast.10), custom_call_target="tpu_custom_call" | custom-call | tf_op jit(solution)/shard_map/finish/pallas_call | solution.py:471
  (65 shorter events, 18.7 us)
Async XLA Ops:
  0.6 46.9 %copy-start = (bf16[4,128,512]{2,1,0:T(8,128)(2,1)S(1)}, bf16[4,128,512]{2,1,0:T(8,128)(2,1)}, u32[]{:S(2)}) copy-start(bf16[4,128,512]{2,1,0:T(8,128)(2,1)} %kv_hbm) | copy-start | bytes 1572868
  0.6 60.9 %copy-start.5 = (s32[128]{0:T(128)S(1)}, s32[128]{0:T(128)}, u32[]{:S(2)}) copy-start(s32[128]{0:T(128)} %param.13) | copy-start | bytes 1540
  0.7 59.2 %copy-start.6 = (s32[128,16]{0,1:T(8,128)S(1)}, s32[128,16]{0,1:T(8,128)}, u32[]{:S(2)}) copy-start(s32[128,16]{0,1:T(8,128)} %param.12) | copy-start | bytes 24580
  2.8 27.4 %all-to-all-start = ((bf16[8,288,128]{2,1,0:T(8,128)(2,1)}), bf16[8,288,128]{2,1,0:T(8,128)(2,1)S(1)}, u32[]{:S(2)}, u32[]{:S(2)}) async-start(bf16[8,288,128]{2,1,0:T(8,128)(2,1)} %bitcast.14), calls=%async_computation | async-start | bytes 1179648 | tf_op jit(solution)/shard_map/all_to_all | solution.py:511
  12.8 5.6 %collective-permute-start.2 = (s32[32]{0:T(128)S(1)}, s32[32]{0:T(128)S(1)}, u32[]{:S(2)}, u32[]{:S(2)}) collective-permute-start(s32[32]{0:T(128)S(1)} %select_reduce_fusion.refs_0_.want_ref), channel_id=1, source_target_pairs={{0,8},{8,16},{16,24},{24,0},{32,40},{40,48},{48,56},{56,32},{64,72... | collective-permute-start | bytes 392 | tf_op jit(solution)/shard_map/ppermute | solution.py:490
  14.5 5.0 %collective-permute-start.1 = (s32[32]{0:T(128)S(1)}, s32[32]{0:T(128)S(1)}, u32[]{:S(2)}, u32[]{:S(2)}) collective-permute-start(s32[32]{0:T(128)S(1)} %select_reduce_fusion.refs_0_.want_ref), channel_id=1, source_target_pairs={{0,16},{8,24},{16,0},{24,8},{32,48},{40,56},{48,32},{56,40},{64,80... | collective-permute-start | bytes 392 | tf_op jit(solution)/shard_map/ppermute | solution.py:490
  15.4 4.1 %collective-permute-start = (s32[32]{0:T(128)S(1)}, s32[32]{0:T(128)S(1)}, u32[]{:S(2)}, u32[]{:S(2)}) collective-permute-start(s32[32]{0:T(128)S(1)} %select_reduce_fusion.refs_0_.want_ref), channel_id=1, source_target_pairs={{0,24},{8,0},{16,8},{24,16},{32,56},{40,32},{48,40},{56,48},{64,88... | collective-permute-start | bytes 392 | tf_op jit(solution)/shard_map/ppermute | solution.py:490
  31.1 6.3 %collective-permute-start.3 = (bf16[576,128]{1,0:T(8,128)(2,1)S(1)}, bf16[576,128]{1,0:T(8,128)(2,1)S(1)}, u32[]{:S(2)}, u32[]{:S(2)}) collective-permute-start(bf16[576,128]{1,0:T(8,128)(2,1)S(1)} %get-tuple-element.58), channel_id=1, source_target_pairs={{0,8},{8,16},{16,24},{24,0},{32,40},{40,48},{48,56},{56,32},{64,72... | collective-permute-start | bytes 442376 | tf_op jit(solution)/shard_map/ppermute | solution.py:490
  32.7 8.3 %collective-permute-start.4 = (bf16[576,128]{1,0:T(8,128)(2,1)S(1)}, bf16[576,128]{1,0:T(8,128)(2,1)S(1)}, u32[]{:S(2)}, u32[]{:S(2)}) collective-permute-start(bf16[576,128]{1,0:T(8,128)(2,1)S(1)} %get-tuple-element.59), channel_id=1, source_target_pairs={{0,16},{8,24},{16,0},{24,8},{32,48},{40,56},{48,32},{56,40},{64,80... | collective-permute-start | bytes 442376 | tf_op jit(solution)/shard_map/ppermute | solution.py:490
  33.7 8.5 %collective-permute-start.5 = (bf16[576,128]{1,0:T(8,128)(2,1)S(1)}, bf16[576,128]{1,0:T(8,128)(2,1)S(1)}, u32[]{:S(2)}, u32[]{:S(2)}) collective-permute-start(bf16[576,128]{1,0:T(8,128)(2,1)S(1)} %get-tuple-element.60), channel_id=1, source_target_pairs={{0,24},{8,0},{16,8},{24,16},{32,56},{40,32},{48,40},{56,48},{64,88... | collective-permute-start | bytes 442376 | tf_op jit(solution)/shard_map/ppermute | solution.py:490
  43.0 12.6 %collective-permute-start.8 = (bf16[944,128]{1,0:T(8,128)(2,1)S(1)}, bf16[944,128]{1,0:T(8,128)(2,1)S(1)}, u32[]{:S(2)}, u32[]{:S(2)}) collective-permute-start(bf16[944,128]{1,0:T(8,128)(2,1)S(1)} %pick_selected.1.x0), channel_id=1, source_target_pairs={{0,6},{1,7},{2,0},{3,1},{4,2},{5,3},{6,4},{7,5},{8,14},{9,15},{10,... | collective-permute-start | bytes 725000 | tf_op jit(solution)/shard_map/ppermute | solution.py:496
  45.9 10.3 %collective-permute-start.7 = (bf16[944,128]{1,0:T(8,128)(2,1)S(1)}, bf16[944,128]{1,0:T(8,128)(2,1)S(1)}, u32[]{:S(2)}, u32[]{:S(2)}) collective-permute-start(bf16[944,128]{1,0:T(8,128)(2,1)S(1)} %pick_selected.1.x0), channel_id=1, source_target_pairs={{0,4},{1,5},{2,6},{3,7},{4,0},{5,1},{6,2},{7,3},{8,12},{9,13},{10,... | collective-permute-start | bytes 725000 | tf_op jit(solution)/shard_map/ppermute | solution.py:496
  46.7 12.7 %collective-permute-start.6 = (bf16[944,128]{1,0:T(8,128)(2,1)S(1)}, bf16[944,128]{1,0:T(8,128)(2,1)S(1)}, u32[]{:S(2)}, u32[]{:S(2)}) collective-permute-start(bf16[944,128]{1,0:T(8,128)(2,1)S(1)} %pick_selected.1.x0), channel_id=1, source_target_pairs={{0,2},{1,3},{2,4},{3,5},{4,6},{5,7},{6,0},{7,1},{8,10},{9,11},{10,... | collective-permute-start | bytes 725000 | tf_op jit(solution)/shard_map/ppermute | solution.py:496
  47.6 12.5 %collective-permute-start.9 = (bf16[944,128]{1,0:T(8,128)(2,1)S(1)}, bf16[944,128]{1,0:T(8,128)(2,1)S(1)}, u32[]{:S(2)}, u32[]{:S(2)}) collective-permute-start(bf16[944,128]{1,0:T(8,128)(2,1)S(1)} %pick_selected.1.x0), channel_id=1, source_target_pairs={{0,1},{1,0},{2,3},{3,2},{4,5},{5,4},{6,7},{7,6},{8,9},{9,8},{10,11... | collective-permute-start | bytes 725000 | tf_op jit(solution)/shard_map/ppermute | solution.py:500
  59.3 1.5 %collective-permute-start.10 = (bf16[944,128]{1,0:T(8,128)(2,1)S(1)}, bf16[944,128]{1,0:T(8,128)(2,1)S(1)}, u32[]{:S(2)}, u32[]{:S(2)}) collective-permute-start(bf16[944,128]{1,0:T(8,128)(2,1)S(1)} %collective-permute-done.6.x1), channel_id=1, source_target_pairs={{0,1},{1,0},{2,3},{3,2},{4,5},{5,4},{6,7},{7,6},{8,9},{9,8},{10,11... | collective-permute-start | bytes 725000 | tf_op jit(solution)/shard_map/ppermute | solution.py:500
  59.3 1.8 %collective-permute-start.11 = (bf16[944,128]{1,0:T(8,128)(2,1)S(1)}, bf16[944,128]{1,0:T(8,128)(2,1)S(1)}, u32[]{:S(2)}, u32[]{:S(2)}) collective-permute-start(bf16[944,128]{1,0:T(8,128)(2,1)S(1)} %collective-permute-done.7.x2), channel_id=1, source_target_pairs={{0,1},{1,0},{2,3},{3,2},{4,5},{5,4},{6,7},{7,6},{8,9},{9,8},{10,11... | collective-permute-start | bytes 725000 | tf_op jit(solution)/shard_map/ppermute | solution.py:500
  59.8 1.7 %collective-permute-start.12 = (bf16[944,128]{1,0:T(8,128)(2,1)S(1)}, bf16[944,128]{1,0:T(8,128)(2,1)S(1)}, u32[]{:S(2)}, u32[]{:S(2)}) collective-permute-start(bf16[944,128]{1,0:T(8,128)(2,1)S(1)} %collective-permute-done.8.x3), channel_id=1, source_target_pairs={{0,1},{1,0},{2,3},{3,2},{4,5},{5,4},{6,7},{7,6},{8,9},{9,8},{10,11... | collective-permute-start | bytes 725000 | tf_op jit(solution)/shard_map/ppermute | solution.py:500
  72.7 2.3 %collective-permute-start.13 = (bf16[1232,128]{1,0:T(8,128)(2,1)S(1)}, bf16[1232,128]{1,0:T(8,128)(2,1)S(1)}, u32[]{:S(2)}, u32[]{:S(2)}) collective-permute-start(bf16[1232,128]{1,0:T(8,128)(2,1)S(1)} %get-tuple-element.74), channel_id=1, source_target_pairs={{0,1},{1,0},{2,3},{3,2},{4,5},{5,4},{6,7},{7,6},{8,9},{9,8},{10,11... | collective-permute-start | bytes 946184 | tf_op jit(solution)/shard_map/ppermute | solution.py:500
  74.5 3.3 %collective-permute-start.14 = (bf16[1232,128]{1,0:T(8,128)(2,1)S(1)}, bf16[1232,128]{1,0:T(8,128)(2,1)S(1)}, u32[]{:S(2)}, u32[]{:S(2)}) collective-permute-start(bf16[1232,128]{1,0:T(8,128)(2,1)S(1)} %get-tuple-element.77), channel_id=1, source_target_pairs={{0,1},{1,0},{2,3},{3,2},{4,5},{5,4},{6,7},{7,6},{8,9},{9,8},{10,11... | collective-permute-start | bytes 946184 | tf_op jit(solution)/shard_map/ppermute | solution.py:500
  75.0 12.5 %collective-permute-start.18 = (bf16[1232,128]{1,0:T(8,128)(2,1)S(1)}, bf16[1232,128]{1,0:T(8,128)(2,1)S(1)}, u32[]{:S(2)}, u32[]{:S(2)}) collective-permute-start(bf16[1232,128]{1,0:T(8,128)(2,1)S(1)} %add_convert_fusion.2), channel_id=1, source_target_pairs={{0,4},{1,5},{2,6},{3,7},{4,0},{5,1},{6,2},{7,3},{8,12},{9,13},{10,... | collective-permute-start | bytes 946184 | tf_op jit(solution)/shard_map/ppermute | solution.py:496
  77.7 3.4 %collective-permute-start.15 = (bf16[1232,128]{1,0:T(8,128)(2,1)S(1)}, bf16[1232,128]{1,0:T(8,128)(2,1)S(1)}, u32[]{:S(2)}, u32[]{:S(2)}) collective-permute-start(bf16[1232,128]{1,0:T(8,128)(2,1)S(1)} %get-tuple-element.83), channel_id=1, source_target_pairs={{0,1},{1,0},{2,3},{3,2},{4,5},{5,4},{6,7},{7,6},{8,9},{9,8},{10,11... | collective-permute-start | bytes 946184 | tf_op jit(solution)/shard_map/ppermute | solution.py:500
  77.9 13.2 %collective-permute-start.17 = (bf16[1232,128]{1,0:T(8,128)(2,1)S(1)}, bf16[1232,128]{1,0:T(8,128)(2,1)S(1)}, u32[]{:S(2)}, u32[]{:S(2)}) collective-permute-start(bf16[1232,128]{1,0:T(8,128)(2,1)S(1)} %add_convert_fusion.1), channel_id=1, source_target_pairs={{0,6},{1,7},{2,0},{3,1},{4,2},{5,3},{6,4},{7,5},{8,14},{9,15},{10,... | collective-permute-start | bytes 946184 | tf_op jit(solution)/shard_map/ppermute | solution.py:496
  80.8 10.3 %collective-permute-start.16 = (bf16[1232,128]{1,0:T(8,128)(2,1)S(1)}, bf16[1232,128]{1,0:T(8,128)(2,1)S(1)}, u32[]{:S(2)}, u32[]{:S(2)}) collective-permute-start(bf16[1232,128]{1,0:T(8,128)(2,1)S(1)} %get-tuple-element.90), channel_id=1, source_target_pairs={{0,1},{1,0},{2,3},{3,2},{4,5},{5,4},{6,7},{7,6},{8,9},{9,8},{10,11... | collective-permute-start | bytes 946184 | tf_op jit(solution)/shard_map/ppermute | solution.py:500
  81.2 11.9 %collective-permute-start.19 = (bf16[1232,128]{1,0:T(8,128)(2,1)S(1)}, bf16[1232,128]{1,0:T(8,128)(2,1)S(1)}, u32[]{:S(2)}, u32[]{:S(2)}) collective-permute-start(bf16[1232,128]{1,0:T(8,128)(2,1)S(1)} %add_convert_fusion), channel_id=1, source_target_pairs={{0,2},{1,3},{2,4},{3,5},{4,6},{5,7},{6,0},{7,1},{8,10},{9,11},{10,... | collective-permute-start | bytes 946184 | tf_op jit(solution)/shard_map/ppermute | solution.py:496
  (4 other events, 95.6 us)

commit v2 on v1

--- a/solution.py
+++ b/solution.py
@@ -257,70 +257,156 @@
     )(src, *cols)
 
 
-def scores_body(me_ref, far_ref, pos_ref, x0, x1, x2, x3, c0, c1, c2, c3, own, q_ref, g_ref,
-                k_out, p_out, ds_out, s_scr, e_scr, bias_scr):
-    me = me_ref[0]
-    pos = pos_ref[...] - me_ref[1]
-    for u in range(REMOTE):
-        line = jnp.broadcast_to(far_ref[u:u + 1, :], (SHARE, 128))
-        for g in range(GROUPS):
-            bias_scr[g * GROUP + u * SHARE:g * GROUP + (u + 1) * SHARE, :] = line
-    step = lax.broadcasted_iota(jnp.int32, (SHARE, 128), 0)
-    for g in range(GROUPS):
-        chip, core = share_of(me, g)
-        for b in range(OWN):
-            at = g * GROUP + FAR_ROWS + b * SHARE
-            key = step + (b * 128 + (chip * 2 + core) * SHARE)
-            bias_scr[at:at + SHARE, :] = jnp.where(key <= pos, 0.0, NEG_FILL)
-    for g, ref in enumerate((x0, c0, x1, c1, x2, c2, x3, c3)):
+def log_scores(keys, q, bias):
+    s = nt_dot(keys, q) * (SCALE_FACTOR * LOG2E)
+    return s + jnp.concatenate([bias, bias], axis=1)
+
+
+def fill_far(refs, k_out, starts):
+    for ref, start in zip(refs, starts):
         for u in range(REMOTE):
-            rows = slice(g * GROUP + u * SHARE, g * GROUP + (u + 1) * SHARE)
+            rows = slice(start + u * SHARE, start + (u + 1) * SHARE)
             for t in range(TILES):
                 at = u * BLOCK_ROWS + t * SHARE
                 k_out[rows, t * 128:(t + 1) * 128] = ref[at:at + SHARE, :]
             at = FAR_LAT + u // 2 * SHARE
             k_out[rows, LAT:] = left_lanes(half_tile(ref[at:at + SHARE, :], u % 2)).astype(BF)
-        k_out[g * GROUP + FAR_ROWS:(g + 1) * GROUP, :] = own[g]
-
-    def chunk(c, carry):
-        at = c * CH
-        q = q_ref[pl.ds(at, CH), :]
-        g = g_ref[pl.ds(at, CH), :]
+
+
+def fill_far_bias(far_ref, bias_scr):
+    for u in range(REMOTE):
+        bias_scr[u * SHARE:(u + 1) * SHARE, :] = jnp.broadcast_to(
+            far_ref[u:u + 1, :], (SHARE, 128)
+        )
+
+
+def far_scores_body(far_ref, x_ref, c_ref, q_ref, k_out, s_out, top_out, bias_scr):
+    fill_far((x_ref, c_ref), k_out, (0, FAR_ROWS))
+    fill_far_bias(far_ref, bias_scr)
+    for c in range(NCH):
+        q = q_ref[c * CH:(c + 1) * CH, :]
         top = jnp.full((1, CH), -jnp.inf, F32)
-        for k in range(GROUPS):
-            rows = slice(k * GROUP, (k + 1) * GROUP)
-            bias = bias_scr[rows, :]
-            s = nt_dot(k_out[rows, :], q) * (SCALE_FACTOR * LOG2E)
-            s = s + jnp.concatenate([bias, bias], axis=1)
-            s_scr[rows, :] = s
+        for cr in range(2):
+            rows = slice(cr * FAR_ROWS, (cr + 1) * FAR_ROWS)
+            s = log_scores(k_out[rows, :], q, bias_scr[...])
+            s_out[c, rows, :] = s
             top = jnp.maximum(top, jnp.max(s, axis=0, keepdims=True))
+        top_out[c] = top
+
+
+def far_scores_call(far, x, c, q):
+    return pl.pallas_call(
+        far_scores_body,
+        in_specs=[vspec()] * 4,
+        out_specs=[vspec()] * 3,
+        out_shape=[
+            jax.ShapeDtypeStruct((2 * FAR_ROWS, WIDE), BF),
+            jax.ShapeDtypeStruct((NCH, 2 * FAR_ROWS, CH), F32),
+            jax.ShapeDtypeStruct((NCH, 1, CH), F32),
+        ],
+        scratch_shapes=[pltpu.VMEM((FAR_ROWS, 128), F32)],
+        compiler_params=params(10),
+        cost_estimate=cost(2 * 2 * FAR_ROWS * ROWS * 640, 4_000_000),
+        name="far_scores",
+    )(far, x, c, q)
+
+
+def own_scores_body(me_ref, pos_ref, own_ref, q_ref, s_out, top_out, bias_scr):
+    pos = pos_ref[...] - me_ref[1]
+    step = lax.broadcasted_iota(jnp.int32, (SHARE, 128), 0)
+    for g in range(GROUPS):
+        chip, core = share_of(me_ref[0], g)
+        for b in range(OWN):
+            at = g * SPAN + b * SHARE
+            key = step + (b * 128 + (chip * 2 + core) * SHARE)
+            bias_scr[at:at + SHARE, :] = jnp.where(key <= pos, 0.0, NEG_FILL)
+    for c in range(NCH):
+        q = q_ref[c * CH:(c + 1) * CH, :]
+        top = jnp.full((1, CH), -jnp.inf, F32)
+        for n in range(2):
+            rows = slice(n * 4 * SPAN, (n + 1) * 4 * SPAN)
+            keys = own_ref[4 * n:4 * n + 4].reshape(4 * SPAN, WIDE)
+            s = log_scores(keys, q, bias_scr[rows, :])
+            s_out[c, rows, :] = s
+            top = jnp.maximum(top, jnp.max(s, axis=0, keepdims=True))
+        top_out[c] = top
+
+
+def own_scores_call(me, pos, own, q):
+    return pl.pallas_call(
+        own_scores_body,
+        in_specs=[pl.BlockSpec(memory_space=pltpu.SMEM)] + [vspec()] * 3,
+        out_specs=[vspec()] * 2,
+        out_shape=[
+            jax.ShapeDtypeStruct((NCH, GROUPS * SPAN, CH), F32),
+            jax.ShapeDtypeStruct((NCH, 1, CH), F32),
+        ],
+        scratch_shapes=[pltpu.VMEM((GROUPS * SPAN, 128), F32)],
+        compiler_params=params(10),
+        cost_estimate=cost(2 * GROUPS * SPAN * ROWS * 640, 4_000_000),
+        name="own_scores",
+    )(me, pos, own, q)
+
+
+EARLY = (0,)
+LATE = tuple(dx for dx in range(NX) if dx not in EARLY)
+
+
+def scores_body(far_ref, own, own_s, own_top, *refs):
+    done = {dx: refs[3 * n:3 * n + 3] for n, dx in enumerate(EARLY)}
+    refs = refs[3 * len(EARLY):]
+    late = {dx: refs[2 * n:2 * n + 2] for n, dx in enumerate(LATE)}
+    q_ref, g_ref, k_out, p_out, ds_out, s_scr, e_scr, bias_scr = refs[2 * len(LATE):]
+    fill_far_bias(far_ref, bias_scr)
+    for g in range(GROUPS):
+        at, dx, cr = g * GROUP, g // 2, g % 2
+        if dx in done:
+            k_out[at:at + FAR_ROWS, :] = done[dx][0][cr * FAR_ROWS:(cr + 1) * FAR_ROWS, :]
+        else:
+            fill_far(late[dx][cr:cr + 1], k_out, (at,))
+        k_out[at + FAR_ROWS:at + GROUP, :] = own[g]
+
+    for c in range(NCH):
+        q = q_ref[c * CH:(c + 1) * CH, :]
+        grad = g_ref[c * CH:(c + 1) * CH, :]
+        top = own_top[c]
+        for dx in EARLY:
+            top = jnp.maximum(top, done[dx][2][c])
+        for dx in LATE:
+            for g in (2 * dx, 2 * dx + 1):
+                rows = slice(g * GROUP, g * GROUP + FAR_ROWS)
+                s = log_scores(k_out[rows, :], q, bias_scr[...])
+                s_scr[rows, :] = s
+                top = jnp.maximum(top, jnp.max(s, axis=0, keepdims=True))
         total = jnp.zeros((1, CH), F32)
         delta = jnp.zeros((1, CH), F32)
-        for k in range(GROUPS):
-            rows = slice(k * GROUP, (k + 1) * GROUP)
-            e = nt_dot(k_out[rows, :LAT], g)
+        for g in range(GROUPS):
+            at, dx, cr = g * GROUP, g // 2, g % 2
+            rows = slice(at, at + GROUP)
+            e = nt_dot(k_out[rows, :LAT], grad)
             e_scr[rows, :] = e
-            w = jnp.exp2(s_scr[rows, :] - top)
+            if dx in done:
+                far = done[dx][1][c, cr * FAR_ROWS:(cr + 1) * FAR_ROWS, :]
+            else:
+                far = s_scr[at:at + FAR_ROWS, :]
+            s = jnp.concatenate([far, own_s[c, g * SPAN:(g + 1) * SPAN, :]], axis=0)
+            w = jnp.exp2(s - top)
             s_scr[rows, :] = w
             total = total + jnp.sum(w, axis=0, keepdims=True)
             delta = delta + jnp.sum(w * e, axis=0, keepdims=True)
         inv = 1.0 / total
         delta = delta * inv
-        for k in range(GROUPS):
-            rows = slice(k * GROUP, (k + 1) * GROUP)
+        for g in range(GROUPS):
+            rows = slice(g * GROUP, (g + 1) * GROUP)
             p = s_scr[rows, :] * inv
             p_out[c, rows, :] = p.astype(BF)
             ds_out[c, rows, :] = ((e_scr[rows, :] - delta) * (p * SCALE_FACTOR)).astype(BF)
-        return carry
-
-    for c in range(NCH):
-        chunk(c, 0)
-
-
-def scores_call(me, far, pos, xs, cs, own, q, g):
+
+
+def scores_call(far, own, own_s, own_top, parts, q, g):
     return pl.pallas_call(
         scores_body,
-        in_specs=[pl.BlockSpec(memory_space=pltpu.SMEM)] + [vspec()] * 13,
+        in_specs=[vspec()] * (4 + len(parts) + 2),
         out_specs=[vspec()] * 3,
         out_shape=[
             jax.ShapeDtypeStruct((KEYS, WIDE), BF),
@@ -330,12 +416,12 @@
         scratch_shapes=[
             pltpu.VMEM((KEYS, CH), F32),
             pltpu.VMEM((KEYS, CH), F32),
-            pltpu.VMEM((KEYS, 128), F32),
+            pltpu.VMEM((FAR_ROWS, 128), F32),
         ],
         compiler_params=params(30),
         cost_estimate=cost(2 * KEYS * ROWS * 1152, 16_000_000),
         name="scores",
-    )(me, far, pos, *xs, *cs, own, q, g)
+    )(far, own, own_s, own_top, *parts, q, g)
 
 
 def dkv_body(p_ref, ds_ref, q_ref, g_ref, keep_ref, send_ref):
@@ -539,9 +625,13 @@
     xs = [x0, x1, x2, x3]
     arrays = after((kv_latent, key_rope, q_latent, q_rope, out_grad), x0)
     own_keys, q, g = prep_call(*arrays)
-    cs = [swap_core(x0)] + [swap_core(after(a, own_keys)) for a in xs[1:]]
-
-    keys, p, ds = scores_call(me, far_bias, query_pos.reshape(1, -1), xs, cs, own_keys, q, g)
+    own_s, own_top = own_scores_call(me, query_pos.reshape(1, -1), own_keys, q)
+
+    parts = list(far_scores_call(far_bias, x0, swap_core(x0), q))
+    xs[1:] = after(xs[1:], own_top, parts[2])
+    for dx in LATE:
+        parts += [xs[dx], swap_core(xs[dx])]
+    keys, p, ds = scores_call(far_bias, own_keys, own_s, own_top, parts, q, g)
 
     order = (2, 1, 3, 0)
     keep, send, part, got = {}, {}, {}, {}

time: 120 us -> 118 us (0.983)
  waiting for transfers between devices: 33.7 us -> 30.9 us
  local copies, waits for them, and re-layouts: 2.89 us -> 1.16 us
  other arithmetic: 1.51 us -> 2.98 us
    unnamed x14, local copies, waits for them, and re-layouts: 1.76 us -> 0.03 us
    ppermute x6, waiting for transfers between devices: 14.3 us -> 13 us  [step_x(): lax.ppermute(a, 'head', [(i, (i + 2 * d) % (2 * NX)) for i in range(2 * N...]
    pallas_call x1 -> x3, Pallas kernels: 9.52 us -> 10.6 us  [the longest x1 7.89 us: scores_call(): pl.pallas_call(scores_body, in_specs=[vspec()] * (4 + len(parts) + 2), ou...]
  transfers between devices with their start and end apart: 21 -> 21, of which waited for: 13 -> 12; matrix products, arithmetic and copies ran while one was open for 2% -> 3% of each run, Pallas kernels for 10% -> 12%
where the time goes in v2:
time: 118 us
  waiting for transfers between devices  30.9 us (26%)
  Pallas kernels  29.8 us (25%)
  starting transfers between devices  27.9 us (24%)
  blocking collectives  24.1 us (20%)
  other arithmetic  2.98 us (3%)
    all_to_all x1, blocking collectives, local(): back = lax.all_to_all(slots, 'ctx', split_axis=0, concat_axis=0, tiled=True)  24.1 us
    ppermute x6, waiting for transfers between devices, step_x(): lax.ppermute(a, 'head', [(i, (i + 2 * d) % (2 * NX)) for i in range(2 * N...  13 us
    all_to_all x1, waiting for transfers between devices, local(): lax.all_to_all(shard, 'ctx', 0, 0, tiled=True, axis_index_groups=columns)  10.2 us
    ppermute x6, starting transfers between devices, step_y(): lax.ppermute(a, 'ctx', [(z * NY + y, z * NY + (y + d) % NY) for z in rang...  10 us
    all_to_all x1, starting transfers between devices, local(): lax.all_to_all(shard, 'ctx', 0, 0, tiled=True, axis_index_groups=columns)  8.48 us
    pallas_call x1, Pallas kernels, scores_call(): pl.pallas_call(scores_body, in_specs=[vspec()] * (4 + len(parts) + 2), ou...  7.89 us
    ppermute x6, starting transfers between devices, step_x(): lax.ppermute(a, 'head', [(i, (i + 2 * d) % (2 * NX)) for i in range(2 * N...  7.59 us
    pallas_call x4, Pallas kernels, dkv_call(): pl.pallas_call(dkv_body, grid=(1,), in_specs=[part, part, pl.BlockSpec((R...  6.45 us
  transfers between devices with their start and end apart: 21, of which 12 were waited for; matrix products, arithmetic and copies ran while one was open for 3% of the time, Pallas kernels for 12%

profile of v2, /device:TPU:8, one launch (start us, length us, event | category | flops | bytes accessed | tf_op | source)
XLA Modules:
  0.0 117.7 jit_solution(16504564673140609791)
XLA Ops:
  0.7 2.1 %pack_share.1 = bf16[2304,128]{1,0:T(8,128)(2,1)} custom-call(bf16[4,128,512]{2,1,0:T(8,128)(2,1)} %kv_hbm, bf16[4,64,128]{2,1,0:T(8,128)(2,1)} %rope_hbm), custom_call_target="tpu_custom_call" | custom-call | tf_op jit(solution)/shard_map/pack_share/pallas_call | solution.py:117
  2.8 8.5 %all-to-all-start = ((bf16[8,288,128]{2,1,0:T(8,128)(2,1)}), bf16[8,288,128]{2,1,0:T(8,128)(2,1)S(1)}, u32[]{:S(2)}, u32[]{:S(2)}) async-start(bf16[8,288,128]{2,1,0:T(8,128)(2,1)} %bitcast.14), calls=%async_computation | async-start | bytes 1179648 | tf_op jit(solution)/shard_map/all_to_all | solution.py:597
  12.9 1.7 %collective-permute-start.2 = (s32[32]{0:T(128)S(1)}, s32[32]{0:T(128)S(1)}, u32[]{:S(2)}, u32[]{:S(2)}) collective-permute-start(s32[32]{0:T(128)S(1)} %select_reduce_fusion.refs_0_.want_ref), channel_id=1, source_target_pairs={{0,8},{8,16},{16,24},{24,0},{32,40},{40,48},{48,56},{56,32},{64,72... | collective-permute-start | bytes 392 | tf_op jit(solution)/shard_map/ppermute | solution.py:576
  15.5 2.4 %collective-permute-start = (s32[32]{0:T(128)S(1)}, s32[32]{0:T(128)S(1)}, u32[]{:S(2)}, u32[]{:S(2)}) collective-permute-start(s32[32]{0:T(128)S(1)} %select_reduce_fusion.refs_0_.want_ref), channel_id=1, source_target_pairs={{0,24},{8,0},{16,8},{24,16},{32,56},{40,32},{48,40},{56,48},{64,88... | collective-permute-start | bytes 392 | tf_op jit(solution)/shard_map/ppermute | solution.py:576
  19.9 10.2 %all-to-all-done = bf16[8,288,128]{2,1,0:T(8,128)(2,1)S(1)} async-done(((bf16[8,288,128]{2,1,0:T(8,128)(2,1)}), bf16[8,288,128]{2,1,0:T(8,128)(2,1)S(1)}, u32[]{:S(2)}, u32[]{:S(2)}) %all-to-all-start) | async-done | bytes 589856 | tf_op jit(solution)/shard_map/all_to_all | solution.py:597
  31.1 1.7 %collective-permute-start.3 = (bf16[576,128]{1,0:T(8,128)(2,1)S(1)}, bf16[576,128]{1,0:T(8,128)(2,1)S(1)}, u32[]{:S(2)}, u32[]{:S(2)}) collective-permute-start(bf16[576,128]{1,0:T(8,128)(2,1)S(1)} %get-tuple-element.61), channel_id=1, source_target_pairs={{0,8},{8,16},{16,24},{24,0},{32,40},{40,48},{48,56},{56,32},{64,72... | collective-permute-start | bytes 442376 | tf_op jit(solution)/shard_map/ppermute | solution.py:576
  33.7 2.4 %collective-permute-start.5 = (bf16[576,128]{1,0:T(8,128)(2,1)S(1)}, bf16[576,128]{1,0:T(8,128)(2,1)S(1)}, u32[]{:S(2)}, u32[]{:S(2)}) collective-permute-start(bf16[576,128]{1,0:T(8,128)(2,1)S(1)} %get-tuple-element.63), channel_id=1, source_target_pairs={{0,24},{8,0},{16,8},{24,16},{32,56},{40,32},{48,40},{56,48},{64,88... | collective-permute-start | bytes 442376 | tf_op jit(solution)/shard_map/ppermute | solution.py:576
  37.4 3.6 %collective-permute-done.4.y2 = bf16[576,128]{1,0:T(8,128)(2,1)S(1)} collective-permute-done((bf16[576,128]{1,0:T(8,128)(2,1)S(1)}, bf16[576,128]{1,0:T(8,128)(2,1)S(1)}, u32[]{:S(2)}, u32[]{:S(2)}) %collective-permute-start.4) | collective-permute-done | bytes 147488 | tf_op jit(solution)/shard_map/ppermute | solution.py:576
  43.1 2.8 %collective-permute-start.9 = (bf16[944,128]{1,0:T(8,128)(2,1)S(1)}, bf16[944,128]{1,0:T(8,128)(2,1)S(1)}, u32[]{:S(2)}, u32[]{:S(2)}) collective-permute-start(bf16[944,128]{1,0:T(8,128)(2,1)S(1)} %pick_selected.1.x_ref), channel_id=1, source_target_pairs={{0,6},{1,7},{2,0},{3,1},{4,2},{5,3},{6,4},{7,5},{8,14},{9,15},{10,... | collective-permute-start | bytes 725000 | tf_op jit(solution)/shard_map/ppermute | solution.py:582
  47.7 1.2 %prep_operands.1 = (bf16[8,64,640]{2,1,0:T(8,128)(2,1)S(1)}, bf16[1024,640]{1,0:T(8,128)(2,1)S(1)}, bf16[1024,512]{1,0:T(8,128)(2,1)S(1)}) custom-call(bf16[4,128,512]{2,1,0:T(8,128)(2,1)S(1)} %copy-done, bf16[4,64,128]{2,1,0:T(8,128)(2,1)S(1)} %copy-done.3, bf16[128,4096]{1,0:T(8,128)(2,1)S(1)} %copy-done.1, bf16[128,512]{1,0:T(8,128)(2,1)S(1)} %copy-done.4, ...), custom_call_target="tpu_custom_call" | custom-call | flops 1000 | bytes 10000000 | tf_op jit(solution)/shard_map/prep_operands/pallas_call | solution.py:177
  48.9 1.6 %own_scores.1 = (f32[4,512,256]{2,1,0:T(8,128)S(1)}, f32[4,1,256]{2,1,0:T(1,128)S(1)}) custom-call(s32[2]{0:T(128)S(1)} %pad_add_fusion.me_ref, s32[1,128]{1,0:T(1,128)S(1)} %bitcast.13, bf16[8,64,640]{2,1,0:T(8,128)(2,1)S(1)} %get-tuple-element.69.own_ref.own, bf16[1024,640]{1,0:T(8,128)(2,1)S(1)} %get-tuple-element.72.q_ref.refs_9_), custom_call_target="tpu_custom_call" | custom-call | flops 671088640 | bytes 4000000 | tf_op jit(solution)/shard_map/own_scores/pallas_call | solution.py:336
  51.6 4.0 %collective-permute-done.9.refs_7_ = bf16[944,128]{1,0:T(8,128)(2,1)S(1)} collective-permute-done((bf16[944,128]{1,0:T(8,128)(2,1)S(1)}, bf16[944,128]{1,0:T(8,128)(2,1)S(1)}, u32[]{:S(2)}, u32[]{:S(2)}) %collective-permute-start.9) | collective-permute-done | bytes 241696 | tf_op jit(solution)/shard_map/ppermute | solution.py:582
  56.2 3.1 %collective-permute-done.7.refs_3_ = bf16[944,128]{1,0:T(8,128)(2,1)S(1)} collective-permute-done((bf16[944,128]{1,0:T(8,128)(2,1)S(1)}, bf16[944,128]{1,0:T(8,128)(2,1)S(1)}, u32[]{:S(2)}, u32[]{:S(2)}) %collective-permute-start.7) | collective-permute-done | bytes 241696 | tf_op jit(solution)/shard_map/ppermute | solution.py:582
  61.5 7.9 %scores.1 = (bf16[2176,640]{1,0:T(8,128)(2,1)S(1)}, bf16[4,2176,256]{2,1,0:T(8,128)(2,1)S(1)}, bf16[4,2176,256]{2,1,0:T(8,128)(2,1)S(1)}) custom-call(f32[16,128]{1,0:T(8,128)S(1)} %select_bitcast_fusion.far_ref, bf16[8,64,640]{2,1,0:T(8,128)(2,1)S(1)} %get-tuple-element.69.own_ref.own, f32[4,512,256]{2,1,0:T(8,128)S(1)} %get-tuple-element.73.own_s, ...), custom_call_target="tpu_custom_call" | custom-call | flops 5133828096 | bytes 16000000 | tf_op jit(solution)/shard_map/scores/pallas_call | solution.py:407
  69.4 1.6 %dkv_chunk2.1 = (f32[1232,128]{1,0:T(8,128)S(1)}, bf16[1232,128]{1,0:T(8,128)(2,1)S(1)}) custom-call(bf16[4,2176,256]{2,1,0:T(8,128)(2,1)S(1)} %get-tuple-element.97.p_ref, bf16[4,2176,256]{2,1,0:T(8,128)(2,1)S(1)} %get-tuple-element.103.ds_ref, bf16[1024,640]{1,0:T(8,128)(2,1)S(1)} %get-tuple-element.72.q_ref.refs_9_, ...), custom_call_target="tpu_custom_call" | custom-call | flops 1283457024 | bytes 5000000 | tf_op jit(solution)/shard_map/dkv_chunk2/pallas_call | solution.py:449
  71.3 1.6 %dkv_chunk1.1 = (f32[1232,128]{1,0:T(8,128)S(1)}, bf16[1232,128]{1,0:T(8,128)(2,1)S(1)}) custom-call(bf16[4,2176,256]{2,1,0:T(8,128)(2,1)S(1)} %get-tuple-element.97.p_ref, bf16[4,2176,256]{2,1,0:T(8,128)(2,1)S(1)} %get-tuple-element.103.ds_ref, bf16[1024,640]{1,0:T(8,128)(2,1)S(1)} %get-tuple-element.72.q_ref.refs_9_, ...), custom_call_target="tpu_custom_call" | custom-call | flops 1283457024 | bytes 5000000 | tf_op jit(solution)/shard_map/dkv_chunk1/pallas_call | solution.py:449
  74.3 1.6 %dkv_chunk3.1 = (f32[1232,128]{1,0:T(8,128)S(1)}, bf16[1232,128]{1,0:T(8,128)(2,1)S(1)}) custom-call(bf16[4,2176,256]{2,1,0:T(8,128)(2,1)S(1)} %get-tuple-element.97.p_ref, bf16[4,2176,256]{2,1,0:T(8,128)(2,1)S(1)} %get-tuple-element.103.ds_ref, bf16[1024,640]{1,0:T(8,128)(2,1)S(1)} %get-tuple-element.72.q_ref.refs_9_, ...), custom_call_target="tpu_custom_call" | custom-call | flops 1283457024 | bytes 5000000 | tf_op jit(solution)/shard_map/dkv_chunk3/pallas_call | solution.py:449
  76.4 1.3 %collective-permute-start.17 = (bf16[1232,128]{1,0:T(8,128)(2,1)S(1)}, bf16[1232,128]{1,0:T(8,128)(2,1)S(1)}, u32[]{:S(2)}, u32[]{:S(2)}) collective-permute-start(bf16[1232,128]{1,0:T(8,128)(2,1)S(1)} %add_convert_fusion.1), channel_id=1, source_target_pairs={{0,6},{1,7},{2,0},{3,1},{4,2},{5,3},{6,4},{7,5},{8,14},{9,15},{10,... | collective-permute-start | bytes 946184 | tf_op jit(solution)/shard_map/ppermute | solution.py:582
  77.7 1.6 %dkv_chunk0.1 = (f32[1232,128]{1,0:T(8,128)S(1)}, bf16[1232,128]{1,0:T(8,128)(2,1)S(1)}) custom-call(bf16[4,2176,256]{2,1,0:T(8,128)(2,1)S(1)} %get-tuple-element.97.p_ref, bf16[4,2176,256]{2,1,0:T(8,128)(2,1)S(1)} %get-tuple-element.103.ds_ref, bf16[1024,640]{1,0:T(8,128)(2,1)S(1)} %get-tuple-element.72.q_ref.refs_9_, ...), custom_call_target="tpu_custom_call" | custom-call | flops 1283457024 | bytes 5000000 | tf_op jit(solution)/shard_map/dkv_chunk0/pallas_call | solution.py:449
  80.7 5.4 %dq.1 = (bf16[128,4096]{1,0:T(8,128)(2,1)}, bf16[128,512]{1,0:T(8,128)(2,1)}) custom-call(bf16[4,2176,256]{2,1,0:T(8,128)(2,1)S(1)} %get-tuple-element.103.ds_ref, bf16[2176,640]{1,0:T(8,128)(2,1)S(1)} %get-tuple-element.104.k_ref), custom_call_target="tpu_custom_call" | custom-call | flops 2852126720 | bytes 8000000 | tf_op jit(solution)/shard_map/dq/pallas_call | solution.py:475
  86.0 3.3 %collective-permute-done.17.r1_ref = bf16[1232,128]{1,0:T(8,128)(2,1)S(1)} collective-permute-done((bf16[1232,128]{1,0:T(8,128)(2,1)S(1)}, bf16[1232,128]{1,0:T(8,128)(2,1)S(1)}, u32[]{:S(2)}, u32[]{:S(2)}) %collective-permute-start.17) | collective-permute-done | bytes 315424 | tf_op jit(solution)/shard_map/ppermute | solution.py:582
  89.3 2.0 %collective-permute-done.19.r3_ref = bf16[1232,128]{1,0:T(8,128)(2,1)S(1)} collective-permute-done((bf16[1232,128]{1,0:T(8,128)(2,1)S(1)}, bf16[1232,128]{1,0:T(8,128)(2,1)S(1)}, u32[]{:S(2)}, u32[]{:S(2)}) %collective-permute-start.19) | collective-permute-done | bytes 315424 | tf_op jit(solution)/shard_map/ppermute | solution.py:582
  92.4 24.1 %all_to_all.22 = bf16[32,16,640]{2,1,0:T(8,128)(2,1)S(1)} all-to-all(bf16[32,16,640]{2,1,0:T(8,128)(2,1)S(1)} %bitcast.12), channel_id=1, replica_groups=mesh['ctx'=32,'head'=8] {'ctx'}, dimensions={0} | all-to-all | bytes 1310720 | tf_op jit(solution)/shard_map/all_to_all | solution.py:651
  116.5 1.3 %finish.1 = (f32[4,16,512]{2,1,0:T(8,128)}, f32[4,8,128]{2,1,0:T(8,128)}) custom-call(f32[64,640]{1,0:T(8,128)S(1)} %get-tuple-element.110.own_ref, bf16[512,640]{1,0:T(8,128)(2,1)S(1)} %bitcast.10), custom_call_target="tpu_custom_call" | custom-call | tf_op jit(solution)/shard_map/finish/pallas_call | solution.py:557
  (67 shorter events, 19.9 us)
Async XLA Ops:
  0.6 47.0 %copy-start.3 = (bf16[4,64,128]{2,1,0:T(8,128)(2,1)S(1)}, bf16[4,64,128]{2,1,0:T(8,128)(2,1)}, u32[]{:S(2)}) copy-start(bf16[4,64,128]{2,1,0:T(8,128)(2,1)} %rope_hbm) | copy-start | bytes 196612
  0.6 47.0 %copy-start = (bf16[4,128,512]{2,1,0:T(8,128)(2,1)S(1)}, bf16[4,128,512]{2,1,0:T(8,128)(2,1)}, u32[]{:S(2)}) copy-start(bf16[4,128,512]{2,1,0:T(8,128)(2,1)} %kv_hbm) | copy-start | bytes 1572868
  0.7 47.0 %copy-start.2 = (bf16[128,4096]{1,0:T(8,128)(2,1)S(1)}, bf16[128,4096]{1,0:T(8,128)(2,1)}, u32[]{:S(2)}) copy-start(bf16[128,4096]{1,0:T(8,128)(2,1)} %g_hbm) | copy-start | bytes 3145732
  2.8 27.4 %all-to-all-start = ((bf16[8,288,128]{2,1,0:T(8,128)(2,1)}), bf16[8,288,128]{2,1,0:T(8,128)(2,1)S(1)}, u32[]{:S(2)}, u32[]{:S(2)}) async-start(bf16[8,288,128]{2,1,0:T(8,128)(2,1)} %bitcast.14), calls=%async_computation | async-start | bytes 1179648 | tf_op jit(solution)/shard_map/all_to_all | solution.py:597
  12.9 7.1 %collective-permute-start.2 = (s32[32]{0:T(128)S(1)}, s32[32]{0:T(128)S(1)}, u32[]{:S(2)}, u32[]{:S(2)}) collective-permute-start(s32[32]{0:T(128)S(1)} %select_reduce_fusion.refs_0_.want_ref), channel_id=1, source_target_pairs={{0,8},{8,16},{16,24},{24,0},{32,40},{40,48},{48,56},{56,32},{64,72... | collective-permute-start | bytes 392 | tf_op jit(solution)/shard_map/ppermute | solution.py:576
  14.5 5.4 %collective-permute-start.1 = (s32[32]{0:T(128)S(1)}, s32[32]{0:T(128)S(1)}, u32[]{:S(2)}, u32[]{:S(2)}) collective-permute-start(s32[32]{0:T(128)S(1)} %select_reduce_fusion.refs_0_.want_ref), channel_id=1, source_target_pairs={{0,16},{8,24},{16,0},{24,8},{32,48},{40,56},{48,32},{56,40},{64,80... | collective-permute-start | bytes 392 | tf_op jit(solution)/shard_map/ppermute | solution.py:576
  15.5 4.5 %collective-permute-start = (s32[32]{0:T(128)S(1)}, s32[32]{0:T(128)S(1)}, u32[]{:S(2)}, u32[]{:S(2)}) collective-permute-start(s32[32]{0:T(128)S(1)} %select_reduce_fusion.refs_0_.want_ref), channel_id=1, source_target_pairs={{0,24},{8,0},{16,8},{24,16},{32,56},{40,32},{48,40},{56,48},{64,88... | collective-permute-start | bytes 392 | tf_op jit(solution)/shard_map/ppermute | solution.py:576
  31.1 6.3 %collective-permute-start.3 = (bf16[576,128]{1,0:T(8,128)(2,1)S(1)}, bf16[576,128]{1,0:T(8,128)(2,1)S(1)}, u32[]{:S(2)}, u32[]{:S(2)}) collective-permute-start(bf16[576,128]{1,0:T(8,128)(2,1)S(1)} %get-tuple-element.61), channel_id=1, source_target_pairs={{0,8},{8,16},{16,24},{24,0},{32,40},{40,48},{48,56},{56,32},{64,72... | collective-permute-start | bytes 442376 | tf_op jit(solution)/shard_map/ppermute | solution.py:576
  32.8 8.3 %collective-permute-start.4 = (bf16[576,128]{1,0:T(8,128)(2,1)S(1)}, bf16[576,128]{1,0:T(8,128)(2,1)S(1)}, u32[]{:S(2)}, u32[]{:S(2)}) collective-permute-start(bf16[576,128]{1,0:T(8,128)(2,1)S(1)} %get-tuple-element.62), channel_id=1, source_target_pairs={{0,16},{8,24},{16,0},{24,8},{32,48},{40,56},{48,32},{56,40},{64,80... | collective-permute-start | bytes 442376 | tf_op jit(solution)/shard_map/ppermute | solution.py:576
  33.7 8.5 %collective-permute-start.5 = (bf16[576,128]{1,0:T(8,128)(2,1)S(1)}, bf16[576,128]{1,0:T(8,128)(2,1)S(1)}, u32[]{:S(2)}, u32[]{:S(2)}) collective-permute-start(bf16[576,128]{1,0:T(8,128)(2,1)S(1)} %get-tuple-element.63), channel_id=1, source_target_pairs={{0,24},{8,0},{16,8},{24,16},{32,56},{40,32},{48,40},{56,48},{64,88... | collective-permute-start | bytes 442376 | tf_op jit(solution)/shard_map/ppermute | solution.py:576
  43.1 12.6 %collective-permute-start.9 = (bf16[944,128]{1,0:T(8,128)(2,1)S(1)}, bf16[944,128]{1,0:T(8,128)(2,1)S(1)}, u32[]{:S(2)}, u32[]{:S(2)}) collective-permute-start(bf16[944,128]{1,0:T(8,128)(2,1)S(1)} %pick_selected.1.x_ref), channel_id=1, source_target_pairs={{0,6},{1,7},{2,0},{3,1},{4,2},{5,3},{6,4},{7,5},{8,14},{9,15},{10,... | collective-permute-start | bytes 725000 | tf_op jit(solution)/shard_map/ppermute | solution.py:582
  45.9 10.3 %collective-permute-start.8 = (bf16[944,128]{1,0:T(8,128)(2,1)S(1)}, bf16[944,128]{1,0:T(8,128)(2,1)S(1)}, u32[]{:S(2)}, u32[]{:S(2)}) collective-permute-start(bf16[944,128]{1,0:T(8,128)(2,1)S(1)} %pick_selected.1.x_ref), channel_id=1, source_target_pairs={{0,4},{1,5},{2,6},{3,7},{4,0},{5,1},{6,2},{7,3},{8,12},{9,13},{10,... | collective-permute-start | bytes 725000 | tf_op jit(solution)/shard_map/ppermute | solution.py:582
  46.7 12.7 %collective-permute-start.7 = (bf16[944,128]{1,0:T(8,128)(2,1)S(1)}, bf16[944,128]{1,0:T(8,128)(2,1)S(1)}, u32[]{:S(2)}, u32[]{:S(2)}) collective-permute-start(bf16[944,128]{1,0:T(8,128)(2,1)S(1)} %pick_selected.1.x_ref), channel_id=1, source_target_pairs={{0,2},{1,3},{2,4},{3,5},{4,6},{5,7},{6,0},{7,1},{8,10},{9,11},{10,... | collective-permute-start | bytes 725000 | tf_op jit(solution)/shard_map/ppermute | solution.py:582
  47.6 3.0 %collective-permute-start.6 = (bf16[944,128]{1,0:T(8,128)(2,1)S(1)}, bf16[944,128]{1,0:T(8,128)(2,1)S(1)}, u32[]{:S(2)}, u32[]{:S(2)}) collective-permute-start(bf16[944,128]{1,0:T(8,128)(2,1)S(1)} %pick_selected.1.x_ref), channel_id=1, source_target_pairs={{0,1},{1,0},{2,3},{3,2},{4,5},{5,4},{6,7},{7,6},{8,9},{9,8},{10,11... | collective-permute-start | bytes 725000 | tf_op jit(solution)/shard_map/ppermute | solution.py:586
  59.3 1.5 %collective-permute-start.10 = (bf16[944,128]{1,0:T(8,128)(2,1)S(1)}, bf16[944,128]{1,0:T(8,128)(2,1)S(1)}, u32[]{:S(2)}, u32[]{:S(2)}) collective-permute-start(bf16[944,128]{1,0:T(8,128)(2,1)S(1)} %collective-permute-done.7.refs_3_), channel_id=1, source_target_pairs={{0,1},{1,0},{2,3},{3,2},{4,5},{5,4},{6,7},{7,6},{8,9},{9,8},{10,11... | collective-permute-start | bytes 725000 | tf_op jit(solution)/shard_map/ppermute | solution.py:586
  59.4 1.8 %collective-permute-start.11 = (bf16[944,128]{1,0:T(8,128)(2,1)S(1)}, bf16[944,128]{1,0:T(8,128)(2,1)S(1)}, u32[]{:S(2)}, u32[]{:S(2)}) collective-permute-start(bf16[944,128]{1,0:T(8,128)(2,1)S(1)} %collective-permute-done.8.refs_5_), channel_id=1, source_target_pairs={{0,1},{1,0},{2,3},{3,2},{4,5},{5,4},{6,7},{7,6},{8,9},{9,8},{10,11... | collective-permute-start | bytes 725000 | tf_op jit(solution)/shard_map/ppermute | solution.py:586
  59.9 1.7 %collective-permute-start.12 = (bf16[944,128]{1,0:T(8,128)(2,1)S(1)}, bf16[944,128]{1,0:T(8,128)(2,1)S(1)}, u32[]{:S(2)}, u32[]{:S(2)}) collective-permute-start(bf16[944,128]{1,0:T(8,128)(2,1)S(1)} %collective-permute-done.9.refs_7_), channel_id=1, source_target_pairs={{0,1},{1,0},{2,3},{3,2},{4,5},{5,4},{6,7},{7,6},{8,9},{9,8},{10,11... | collective-permute-start | bytes 725000 | tf_op jit(solution)/shard_map/ppermute | solution.py:586
  71.1 2.3 %collective-permute-start.13 = (bf16[1232,128]{1,0:T(8,128)(2,1)S(1)}, bf16[1232,128]{1,0:T(8,128)(2,1)S(1)}, u32[]{:S(2)}, u32[]{:S(2)}) collective-permute-start(bf16[1232,128]{1,0:T(8,128)(2,1)S(1)} %get-tuple-element.84), channel_id=1, source_target_pairs={{0,1},{1,0},{2,3},{3,2},{4,5},{5,4},{6,7},{7,6},{8,9},{9,8},{10,11... | collective-permute-start | bytes 946184 | tf_op jit(solution)/shard_map/ppermute | solution.py:586
  72.9 3.4 %collective-permute-start.14 = (bf16[1232,128]{1,0:T(8,128)(2,1)S(1)}, bf16[1232,128]{1,0:T(8,128)(2,1)S(1)}, u32[]{:S(2)}, u32[]{:S(2)}) collective-permute-start(bf16[1232,128]{1,0:T(8,128)(2,1)S(1)} %get-tuple-element.87), channel_id=1, source_target_pairs={{0,1},{1,0},{2,3},{3,2},{4,5},{5,4},{6,7},{7,6},{8,9},{9,8},{10,11... | collective-permute-start | bytes 946184 | tf_op jit(solution)/shard_map/ppermute | solution.py:586
  73.5 12.6 %collective-permute-start.18 = (bf16[1232,128]{1,0:T(8,128)(2,1)S(1)}, bf16[1232,128]{1,0:T(8,128)(2,1)S(1)}, u32[]{:S(2)}, u32[]{:S(2)}) collective-permute-start(bf16[1232,128]{1,0:T(8,128)(2,1)S(1)} %add_convert_fusion.2), channel_id=1, source_target_pairs={{0,4},{1,5},{2,6},{3,7},{4,0},{5,1},{6,2},{7,3},{8,12},{9,13},{10,... | collective-permute-start | bytes 946184 | tf_op jit(solution)/shard_map/ppermute | solution.py:582
  76.0 3.6 %collective-permute-start.15 = (bf16[1232,128]{1,0:T(8,128)(2,1)S(1)}, bf16[1232,128]{1,0:T(8,128)(2,1)S(1)}, u32[]{:S(2)}, u32[]{:S(2)}) collective-permute-start(bf16[1232,128]{1,0:T(8,128)(2,1)S(1)} %get-tuple-element.93), channel_id=1, source_target_pairs={{0,1},{1,0},{2,3},{3,2},{4,5},{5,4},{6,7},{7,6},{8,9},{9,8},{10,11... | collective-permute-start | bytes 946184 | tf_op jit(solution)/shard_map/ppermute | solution.py:586
  76.4 12.9 %collective-permute-start.17 = (bf16[1232,128]{1,0:T(8,128)(2,1)S(1)}, bf16[1232,128]{1,0:T(8,128)(2,1)S(1)}, u32[]{:S(2)}, u32[]{:S(2)}) collective-permute-start(bf16[1232,128]{1,0:T(8,128)(2,1)S(1)} %add_convert_fusion.1), channel_id=1, source_target_pairs={{0,6},{1,7},{2,0},{3,1},{4,2},{5,3},{6,4},{7,5},{8,14},{9,15},{10,... | collective-permute-start | bytes 946184 | tf_op jit(solution)/shard_map/ppermute | solution.py:582
  79.3 10.0 %collective-permute-start.16 = (bf16[1232,128]{1,0:T(8,128)(2,1)S(1)}, bf16[1232,128]{1,0:T(8,128)(2,1)S(1)}, u32[]{:S(2)}, u32[]{:S(2)}) collective-permute-start(bf16[1232,128]{1,0:T(8,128)(2,1)S(1)} %get-tuple-element.100), channel_id=1, source_target_pairs={{0,1},{1,0},{2,3},{3,2},{4,5},{5,4},{6,7},{7,6},{8,9},{9,8},{10,11... | collective-permute-start | bytes 946184 | tf_op jit(solution)/shard_map/ppermute | solution.py:586
  79.7 11.6 %collective-permute-start.19 = (bf16[1232,128]{1,0:T(8,128)(2,1)S(1)}, bf16[1232,128]{1,0:T(8,128)(2,1)S(1)}, u32[]{:S(2)}, u32[]{:S(2)}) collective-permute-start(bf16[1232,128]{1,0:T(8,128)(2,1)S(1)} %add_convert_fusion), channel_id=1, source_target_pairs={{0,2},{1,3},{2,4},{3,5},{4,6},{5,7},{6,0},{7,1},{8,10},{9,11},{10,... | collective-permute-start | bytes 946184 | tf_op jit(solution)/shard_map/ppermute | solution.py:582
  (4 other events, 175.6 us)

commit v3 on v2

--- a/solution.py
+++ b/solution.py
@@ -628,9 +628,10 @@
     own_s, own_top = own_scores_call(me, query_pos.reshape(1, -1), own_keys, q)
 
     parts = list(far_scores_call(far_bias, x0, swap_core(x0), q))
-    xs[1:] = after(xs[1:], own_top, parts[2])
-    for dx in LATE:
-        parts += [xs[dx], swap_core(xs[dx])]
+    x2, x3 = after((xs[2], xs[3]), own_top, parts[2])
+    c2, c3 = swap_core(x2), swap_core(x3)
+    x1 = after(xs[1], own_top, parts[2], c2, c3)
+    parts += [x1, swap_core(x1), x2, c2, x3, c3]
     keys, p, ds = scores_call(far_bias, own_keys, own_s, own_top, parts, q, g)
 
     order = (2, 1, 3, 0)

time: 118 us -> 117 us (level)
  transfers between devices with their start and end apart: 21 -> 21, of which waited for: 12 -> 10; matrix products, arithmetic and copies ran while one was open for 3% -> 4% of each run, Pallas kernels for 12% -> 12%
where the time goes in v3:
time: 117 us
  waiting for transfers between devices  30.3 us (26%)
  Pallas kernels  29.8 us (25%)
  starting transfers between devices  28.1 us (24%)
  blocking collectives  23.6 us (20%)
  other arithmetic  2.98 us (3%)
    all_to_all x1, blocking collectives, local(): back = lax.all_to_all(slots, 'ctx', split_axis=0, concat_axis=0, tiled=True)  23.6 us
    ppermute x6, waiting for transfers between devices, step_x(): lax.ppermute(a, 'head', [(i, (i + 2 * d) % (2 * NX)) for i in range(2 * N...  12.6 us
    all_to_all x1, waiting for transfers between devices, local(): lax.all_to_all(shard, 'ctx', 0, 0, tiled=True, axis_index_groups=columns)  10.2 us
    ppermute x6, starting transfers between devices, step_y(): lax.ppermute(a, 'ctx', [(z * NY + y, z * NY + (y + d) % NY) for z in rang...  10 us
    all_to_all x1, starting transfers between devices, local(): lax.all_to_all(shard, 'ctx', 0, 0, tiled=True, axis_index_groups=columns)  8.48 us
    pallas_call x1, Pallas kernels, scores_call(): pl.pallas_call(scores_body, in_specs=[vspec()] * (4 + len(parts) + 2), ou...  7.9 us
    ppermute x6, starting transfers between devices, step_x(): lax.ppermute(a, 'head', [(i, (i + 2 * d) % (2 * NX)) for i in range(2 * N...  7.77 us
    pallas_call x4, Pallas kernels, dkv_call(): pl.pallas_call(dkv_body, grid=(1,), in_specs=[part, part, pl.BlockSpec((R...  6.45 us
  transfers between devices with their start and end apart: 21, of which 10 were waited for; matrix products, arithmetic and copies ran while one was open for 4% of the time, Pallas kernels for 12%

profile of v3, /device:TPU:8, one launch (start us, length us, event | category | flops | bytes accessed | tf_op | source)
XLA Modules:
  0.0 116.9 jit_solution(6195701673697778821)
XLA Ops:
  0.7 2.1 %pack_share.1 = bf16[2304,128]{1,0:T(8,128)(2,1)} custom-call(bf16[4,128,512]{2,1,0:T(8,128)(2,1)} %kv_hbm, bf16[4,64,128]{2,1,0:T(8,128)(2,1)} %rope_hbm), custom_call_target="tpu_custom_call" | custom-call | tf_op jit(solution)/shard_map/pack_share/pallas_call | solution.py:117
  2.8 8.5 %all-to-all-start = ((bf16[8,288,128]{2,1,0:T(8,128)(2,1)}), bf16[8,288,128]{2,1,0:T(8,128)(2,1)S(1)}, u32[]{:S(2)}, u32[]{:S(2)}) async-start(bf16[8,288,128]{2,1,0:T(8,128)(2,1)} %bitcast.14), calls=%async_computation | async-start | bytes 1179648 | tf_op jit(solution)/shard_map/all_to_all | solution.py:597
  12.9 1.7 %collective-permute-start.2 = (s32[32]{0:T(128)S(1)}, s32[32]{0:T(128)S(1)}, u32[]{:S(2)}, u32[]{:S(2)}) collective-permute-start(s32[32]{0:T(128)S(1)} %select_reduce_fusion.refs_0_.want_ref), channel_id=1, source_target_pairs={{0,8},{8,16},{16,24},{24,0},{32,40},{40,48},{48,56},{56,32},{64,72... | collective-permute-start | bytes 392 | tf_op jit(solution)/shard_map/ppermute | solution.py:576
  15.5 2.4 %collective-permute-start = (s32[32]{0:T(128)S(1)}, s32[32]{0:T(128)S(1)}, u32[]{:S(2)}, u32[]{:S(2)}) collective-permute-start(s32[32]{0:T(128)S(1)} %select_reduce_fusion.refs_0_.want_ref), channel_id=1, source_target_pairs={{0,24},{8,0},{16,8},{24,16},{32,56},{40,32},{48,40},{56,48},{64,88... | collective-permute-start | bytes 392 | tf_op jit(solution)/shard_map/ppermute | solution.py:576
  19.9 10.2 %all-to-all-done = bf16[8,288,128]{2,1,0:T(8,128)(2,1)S(1)} async-done(((bf16[8,288,128]{2,1,0:T(8,128)(2,1)}), bf16[8,288,128]{2,1,0:T(8,128)(2,1)S(1)}, u32[]{:S(2)}, u32[]{:S(2)}) %all-to-all-start) | async-done | bytes 589856 | tf_op jit(solution)/shard_map/all_to_all | solution.py:597
  31.1 1.7 %collective-permute-start.3 = (bf16[576,128]{1,0:T(8,128)(2,1)S(1)}, bf16[576,128]{1,0:T(8,128)(2,1)S(1)}, u32[]{:S(2)}, u32[]{:S(2)}) collective-permute-start(bf16[576,128]{1,0:T(8,128)(2,1)S(1)} %get-tuple-element.61), channel_id=1, source_target_pairs={{0,8},{8,16},{16,24},{24,0},{32,40},{40,48},{48,56},{56,32},{64,72... | collective-permute-start | bytes 442376 | tf_op jit(solution)/shard_map/ppermute | solution.py:576
  33.7 2.4 %collective-permute-start.5 = (bf16[576,128]{1,0:T(8,128)(2,1)S(1)}, bf16[576,128]{1,0:T(8,128)(2,1)S(1)}, u32[]{:S(2)}, u32[]{:S(2)}) collective-permute-start(bf16[576,128]{1,0:T(8,128)(2,1)S(1)} %get-tuple-element.63), channel_id=1, source_target_pairs={{0,24},{8,0},{16,8},{24,16},{32,56},{40,32},{48,40},{56,48},{64,88... | collective-permute-start | bytes 442376 | tf_op jit(solution)/shard_map/ppermute | solution.py:576
  37.4 3.6 %collective-permute-done.4.y2 = bf16[576,128]{1,0:T(8,128)(2,1)S(1)} collective-permute-done((bf16[576,128]{1,0:T(8,128)(2,1)S(1)}, bf16[576,128]{1,0:T(8,128)(2,1)S(1)}, u32[]{:S(2)}, u32[]{:S(2)}) %collective-permute-start.4) | collective-permute-done | bytes 147488 | tf_op jit(solution)/shard_map/ppermute | solution.py:576
  43.1 2.8 %collective-permute-start.9 = (bf16[944,128]{1,0:T(8,128)(2,1)S(1)}, bf16[944,128]{1,0:T(8,128)(2,1)S(1)}, u32[]{:S(2)}, u32[]{:S(2)}) collective-permute-start(bf16[944,128]{1,0:T(8,128)(2,1)S(1)} %pick_selected.1.x_ref), channel_id=1, source_target_pairs={{0,6},{1,7},{2,0},{3,1},{4,2},{5,3},{6,4},{7,5},{8,14},{9,15},{10,... | collective-permute-start | bytes 725000 | tf_op jit(solution)/shard_map/ppermute | solution.py:582
  47.7 1.2 %prep_operands.1 = (bf16[8,64,640]{2,1,0:T(8,128)(2,1)S(1)}, bf16[1024,640]{1,0:T(8,128)(2,1)S(1)}, bf16[1024,512]{1,0:T(8,128)(2,1)S(1)}) custom-call(bf16[4,128,512]{2,1,0:T(8,128)(2,1)S(1)} %copy-done, bf16[4,64,128]{2,1,0:T(8,128)(2,1)S(1)} %copy-done.3, bf16[128,4096]{1,0:T(8,128)(2,1)S(1)} %copy-done.1, bf16[128,512]{1,0:T(8,128)(2,1)S(1)} %copy-done.4, ...), custom_call_target="tpu_custom_call" | custom-call | flops 1000 | bytes 10000000 | tf_op jit(solution)/shard_map/prep_operands/pallas_call | solution.py:177
  49.0 1.6 %own_scores.1 = (f32[4,512,256]{2,1,0:T(8,128)S(1)}, f32[4,1,256]{2,1,0:T(1,128)S(1)}) custom-call(s32[2]{0:T(128)S(1)} %pad_add_fusion.me_ref, s32[1,128]{1,0:T(1,128)S(1)} %bitcast.13, bf16[8,64,640]{2,1,0:T(8,128)(2,1)S(1)} %get-tuple-element.69.own_ref.own, bf16[1024,640]{1,0:T(8,128)(2,1)S(1)} %get-tuple-element.72.q_ref.refs_9_), custom_call_target="tpu_custom_call" | custom-call | flops 671088640 | bytes 4000000 | tf_op jit(solution)/shard_map/own_scores/pallas_call | solution.py:336
  51.6 4.0 %collective-permute-done.9.refs_7_ = bf16[944,128]{1,0:T(8,128)(2,1)S(1)} collective-permute-done((bf16[944,128]{1,0:T(8,128)(2,1)S(1)}, bf16[944,128]{1,0:T(8,128)(2,1)S(1)}, u32[]{:S(2)}, u32[]{:S(2)}) %collective-permute-start.9) | collective-permute-done | bytes 241696 | tf_op jit(solution)/shard_map/ppermute | solution.py:582
  56.7 2.6 %collective-permute-done.7.refs_3_ = bf16[944,128]{1,0:T(8,128)(2,1)S(1)} collective-permute-done((bf16[944,128]{1,0:T(8,128)(2,1)S(1)}, bf16[944,128]{1,0:T(8,128)(2,1)S(1)}, u32[]{:S(2)}, u32[]{:S(2)}) %collective-permute-start.7) | collective-permute-done | bytes 241696 | tf_op jit(solution)/shard_map/ppermute | solution.py:582
  59.4 1.4 %collective-permute-done.12.refs_4_ = bf16[944,128]{1,0:T(8,128)(2,1)S(1)} collective-permute-done((bf16[944,128]{1,0:T(8,128)(2,1)S(1)}, bf16[944,128]{1,0:T(8,128)(2,1)S(1)}, u32[]{:S(2)}, u32[]{:S(2)}) %collective-permute-start.12) | collective-permute-done | bytes 241696 | tf_op jit(solution)/shard_map/ppermute | solution.py:586
  60.9 7.9 %scores.1 = (bf16[2176,640]{1,0:T(8,128)(2,1)S(1)}, bf16[4,2176,256]{2,1,0:T(8,128)(2,1)S(1)}, bf16[4,2176,256]{2,1,0:T(8,128)(2,1)S(1)}) custom-call(f32[16,128]{1,0:T(8,128)S(1)} %select_bitcast_fusion.far_ref, bf16[8,64,640]{2,1,0:T(8,128)(2,1)S(1)} %get-tuple-element.69.own_ref.own, f32[4,512,256]{2,1,0:T(8,128)S(1)} %get-tuple-element.73.own_s, ...), custom_call_target="tpu_custom_call" | custom-call | flops 5133828096 | bytes 16000000 | tf_op jit(solution)/shard_map/scores/pallas_call | solution.py:407
  68.8 1.6 %dkv_chunk2.1 = (f32[1232,128]{1,0:T(8,128)S(1)}, bf16[1232,128]{1,0:T(8,128)(2,1)S(1)}) custom-call(bf16[4,2176,256]{2,1,0:T(8,128)(2,1)S(1)} %get-tuple-element.97.p_ref, bf16[4,2176,256]{2,1,0:T(8,128)(2,1)S(1)} %get-tuple-element.103.ds_ref, bf16[1024,640]{1,0:T(8,128)(2,1)S(1)} %get-tuple-element.72.q_ref.refs_9_, ...), custom_call_target="tpu_custom_call" | custom-call | flops 1283457024 | bytes 5000000 | tf_op jit(solution)/shard_map/dkv_chunk2/pallas_call | solution.py:449
  70.6 1.6 %dkv_chunk1.1 = (f32[1232,128]{1,0:T(8,128)S(1)}, bf16[1232,128]{1,0:T(8,128)(2,1)S(1)}) custom-call(bf16[4,2176,256]{2,1,0:T(8,128)(2,1)S(1)} %get-tuple-element.97.p_ref, bf16[4,2176,256]{2,1,0:T(8,128)(2,1)S(1)} %get-tuple-element.103.ds_ref, bf16[1024,640]{1,0:T(8,128)(2,1)S(1)} %get-tuple-element.72.q_ref.refs_9_, ...), custom_call_target="tpu_custom_call" | custom-call | flops 1283457024 | bytes 5000000 | tf_op jit(solution)/shard_map/dkv_chunk1/pallas_call | solution.py:449
  73.7 1.6 %dkv_chunk3.1 = (f32[1232,128]{1,0:T(8,128)S(1)}, bf16[1232,128]{1,0:T(8,128)(2,1)S(1)}) custom-call(bf16[4,2176,256]{2,1,0:T(8,128)(2,1)S(1)} %get-tuple-element.97.p_ref, bf16[4,2176,256]{2,1,0:T(8,128)(2,1)S(1)} %get-tuple-element.103.ds_ref, bf16[1024,640]{1,0:T(8,128)(2,1)S(1)} %get-tuple-element.72.q_ref.refs_9_, ...), custom_call_target="tpu_custom_call" | custom-call | flops 1283457024 | bytes 5000000 | tf_op jit(solution)/shard_map/dkv_chunk3/pallas_call | solution.py:449
  75.7 2.2 %collective-permute-start.17 = (bf16[1232,128]{1,0:T(8,128)(2,1)S(1)}, bf16[1232,128]{1,0:T(8,128)(2,1)S(1)}, u32[]{:S(2)}, u32[]{:S(2)}) collective-permute-start(bf16[1232,128]{1,0:T(8,128)(2,1)S(1)} %add_convert_fusion.1), channel_id=1, source_target_pairs={{0,6},{1,7},{2,0},{3,1},{4,2},{5,3},{6,4},{7,5},{8,14},{9,15},{10,... | collective-permute-start | bytes 946184 | tf_op jit(solution)/shard_map/ppermute | solution.py:582
  77.9 1.6 %dkv_chunk0.1 = (f32[1232,128]{1,0:T(8,128)S(1)}, bf16[1232,128]{1,0:T(8,128)(2,1)S(1)}) custom-call(bf16[4,2176,256]{2,1,0:T(8,128)(2,1)S(1)} %get-tuple-element.97.p_ref, bf16[4,2176,256]{2,1,0:T(8,128)(2,1)S(1)} %get-tuple-element.103.ds_ref, bf16[1024,640]{1,0:T(8,128)(2,1)S(1)} %get-tuple-element.72.q_ref.refs_9_, ...), custom_call_target="tpu_custom_call" | custom-call | flops 1283457024 | bytes 5000000 | tf_op jit(solution)/shard_map/dkv_chunk0/pallas_call | solution.py:449
  80.1 5.3 %dq.1 = (bf16[128,4096]{1,0:T(8,128)(2,1)}, bf16[128,512]{1,0:T(8,128)(2,1)}) custom-call(bf16[4,2176,256]{2,1,0:T(8,128)(2,1)S(1)} %get-tuple-element.103.ds_ref, bf16[2176,640]{1,0:T(8,128)(2,1)S(1)} %get-tuple-element.104.k_ref), custom_call_target="tpu_custom_call" | custom-call | flops 2852126720 | bytes 8000000 | tf_op jit(solution)/shard_map/dq/pallas_call | solution.py:475
  85.5 4.4 %collective-permute-done.17.r1_ref = bf16[1232,128]{1,0:T(8,128)(2,1)S(1)} collective-permute-done((bf16[1232,128]{1,0:T(8,128)(2,1)S(1)}, bf16[1232,128]{1,0:T(8,128)(2,1)S(1)}, u32[]{:S(2)}, u32[]{:S(2)}) %collective-permute-start.17) | collective-permute-done | bytes 315424 | tf_op jit(solution)/shard_map/ppermute | solution.py:582
  92.0 23.6 %all_to_all.22 = bf16[32,16,640]{2,1,0:T(8,128)(2,1)S(1)} all-to-all(bf16[32,16,640]{2,1,0:T(8,128)(2,1)S(1)} %bitcast.12), channel_id=1, replica_groups=mesh['ctx'=32,'head'=8] {'ctx'}, dimensions={0} | all-to-all | bytes 1310720 | tf_op jit(solution)/shard_map/all_to_all | solution.py:652
  115.6 1.3 %finish.1 = (f32[4,16,512]{2,1,0:T(8,128)}, f32[4,8,128]{2,1,0:T(8,128)}) custom-call(f32[64,640]{1,0:T(8,128)S(1)} %get-tuple-element.110.own_ref, bf16[512,640]{1,0:T(8,128)(2,1)S(1)} %bitcast.10), custom_call_target="tpu_custom_call" | custom-call | tf_op jit(solution)/shard_map/finish/pallas_call | solution.py:557
  (67 shorter events, 18.5 us)
Async XLA Ops:
  0.6 47.0 %copy-start.3 = (bf16[4,64,128]{2,1,0:T(8,128)(2,1)S(1)}, bf16[4,64,128]{2,1,0:T(8,128)(2,1)}, u32[]{:S(2)}) copy-start(bf16[4,64,128]{2,1,0:T(8,128)(2,1)} %rope_hbm) | copy-start | bytes 196612
  0.6 47.0 %copy-start = (bf16[4,128,512]{2,1,0:T(8,128)(2,1)S(1)}, bf16[4,128,512]{2,1,0:T(8,128)(2,1)}, u32[]{:S(2)}) copy-start(bf16[4,128,512]{2,1,0:T(8,128)(2,1)} %kv_hbm) | copy-start | bytes 1572868
  0.7 47.0 %copy-start.2 = (bf16[128,4096]{1,0:T(8,128)(2,1)S(1)}, bf16[128,4096]{1,0:T(8,128)(2,1)}, u32[]{:S(2)}) copy-start(bf16[128,4096]{1,0:T(8,128)(2,1)} %g_hbm) | copy-start | bytes 3145732
  2.8 27.4 %all-to-all-start = ((bf16[8,288,128]{2,1,0:T(8,128)(2,1)}), bf16[8,288,128]{2,1,0:T(8,128)(2,1)S(1)}, u32[]{:S(2)}, u32[]{:S(2)}) async-start(bf16[8,288,128]{2,1,0:T(8,128)(2,1)} %bitcast.14), calls=%async_computation | async-start | bytes 1179648 | tf_op jit(solution)/shard_map/all_to_all | solution.py:597
  12.9 7.1 %collective-permute-start.2 = (s32[32]{0:T(128)S(1)}, s32[32]{0:T(128)S(1)}, u32[]{:S(2)}, u32[]{:S(2)}) collective-permute-start(s32[32]{0:T(128)S(1)} %select_reduce_fusion.refs_0_.want_ref), channel_id=1, source_target_pairs={{0,8},{8,16},{16,24},{24,0},{32,40},{40,48},{48,56},{56,32},{64,72... | collective-permute-start | bytes 392 | tf_op jit(solution)/shard_map/ppermute | solution.py:576
  14.5 5.4 %collective-permute-start.1 = (s32[32]{0:T(128)S(1)}, s32[32]{0:T(128)S(1)}, u32[]{:S(2)}, u32[]{:S(2)}) collective-permute-start(s32[32]{0:T(128)S(1)} %select_reduce_fusion.refs_0_.want_ref), channel_id=1, source_target_pairs={{0,16},{8,24},{16,0},{24,8},{32,48},{40,56},{48,32},{56,40},{64,80... | collective-permute-start | bytes 392 | tf_op jit(solution)/shard_map/ppermute | solution.py:576
  15.5 4.5 %collective-permute-start = (s32[32]{0:T(128)S(1)}, s32[32]{0:T(128)S(1)}, u32[]{:S(2)}, u32[]{:S(2)}) collective-permute-start(s32[32]{0:T(128)S(1)} %select_reduce_fusion.refs_0_.want_ref), channel_id=1, source_target_pairs={{0,24},{8,0},{16,8},{24,16},{32,56},{40,32},{48,40},{56,48},{64,88... | collective-permute-start | bytes 392 | tf_op jit(solution)/shard_map/ppermute | solution.py:576
  31.1 6.3 %collective-permute-start.3 = (bf16[576,128]{1,0:T(8,128)(2,1)S(1)}, bf16[576,128]{1,0:T(8,128)(2,1)S(1)}, u32[]{:S(2)}, u32[]{:S(2)}) collective-permute-start(bf16[576,128]{1,0:T(8,128)(2,1)S(1)} %get-tuple-element.61), channel_id=1, source_target_pairs={{0,8},{8,16},{16,24},{24,0},{32,40},{40,48},{48,56},{56,32},{64,72... | collective-permute-start | bytes 442376 | tf_op jit(solution)/shard_map/ppermute | solution.py:576
  32.8 8.3 %collective-permute-start.4 = (bf16[576,128]{1,0:T(8,128)(2,1)S(1)}, bf16[576,128]{1,0:T(8,128)(2,1)S(1)}, u32[]{:S(2)}, u32[]{:S(2)}) collective-permute-start(bf16[576,128]{1,0:T(8,128)(2,1)S(1)} %get-tuple-element.62), channel_id=1, source_target_pairs={{0,16},{8,24},{16,0},{24,8},{32,48},{40,56},{48,32},{56,40},{64,80... | collective-permute-start | bytes 442376 | tf_op jit(solution)/shard_map/ppermute | solution.py:576
  33.7 8.5 %collective-permute-start.5 = (bf16[576,128]{1,0:T(8,128)(2,1)S(1)}, bf16[576,128]{1,0:T(8,128)(2,1)S(1)}, u32[]{:S(2)}, u32[]{:S(2)}) collective-permute-start(bf16[576,128]{1,0:T(8,128)(2,1)S(1)} %get-tuple-element.63), channel_id=1, source_target_pairs={{0,24},{8,0},{16,8},{24,16},{32,56},{40,32},{48,40},{56,48},{64,88... | collective-permute-start | bytes 442376 | tf_op jit(solution)/shard_map/ppermute | solution.py:576
  43.1 12.6 %collective-permute-start.9 = (bf16[944,128]{1,0:T(8,128)(2,1)S(1)}, bf16[944,128]{1,0:T(8,128)(2,1)S(1)}, u32[]{:S(2)}, u32[]{:S(2)}) collective-permute-start(bf16[944,128]{1,0:T(8,128)(2,1)S(1)} %pick_selected.1.x_ref), channel_id=1, source_target_pairs={{0,6},{1,7},{2,0},{3,1},{4,2},{5,3},{6,4},{7,5},{8,14},{9,15},{10,... | collective-permute-start | bytes 725000 | tf_op jit(solution)/shard_map/ppermute | solution.py:582
  45.9 10.3 %collective-permute-start.8 = (bf16[944,128]{1,0:T(8,128)(2,1)S(1)}, bf16[944,128]{1,0:T(8,128)(2,1)S(1)}, u32[]{:S(2)}, u32[]{:S(2)}) collective-permute-start(bf16[944,128]{1,0:T(8,128)(2,1)S(1)} %pick_selected.1.x_ref), channel_id=1, source_target_pairs={{0,4},{1,5},{2,6},{3,7},{4,0},{5,1},{6,2},{7,3},{8,12},{9,13},{10,... | collective-permute-start | bytes 725000 | tf_op jit(solution)/shard_map/ppermute | solution.py:582
  46.7 3.9 %collective-permute-start.6 = (bf16[944,128]{1,0:T(8,128)(2,1)S(1)}, bf16[944,128]{1,0:T(8,128)(2,1)S(1)}, u32[]{:S(2)}, u32[]{:S(2)}) collective-permute-start(bf16[944,128]{1,0:T(8,128)(2,1)S(1)} %pick_selected.1.x_ref), channel_id=1, source_target_pairs={{0,1},{1,0},{2,3},{3,2},{4,5},{5,4},{6,7},{7,6},{8,9},{9,8},{10,11... | collective-permute-start | bytes 725000 | tf_op jit(solution)/shard_map/ppermute | solution.py:586
  46.8 12.6 %collective-permute-start.7 = (bf16[944,128]{1,0:T(8,128)(2,1)S(1)}, bf16[944,128]{1,0:T(8,128)(2,1)S(1)}, u32[]{:S(2)}, u32[]{:S(2)}) collective-permute-start(bf16[944,128]{1,0:T(8,128)(2,1)S(1)} %pick_selected.1.x_ref), channel_id=1, source_target_pairs={{0,2},{1,3},{2,4},{3,5},{4,6},{5,7},{6,0},{7,1},{8,10},{9,11},{10,... | collective-permute-start | bytes 725000 | tf_op jit(solution)/shard_map/ppermute | solution.py:582
  56.2 3.2 %collective-permute-start.10 = (bf16[944,128]{1,0:T(8,128)(2,1)S(1)}, bf16[944,128]{1,0:T(8,128)(2,1)S(1)}, u32[]{:S(2)}, u32[]{:S(2)}) collective-permute-start(bf16[944,128]{1,0:T(8,128)(2,1)S(1)} %collective-permute-done.8.refs_5_), channel_id=1, source_target_pairs={{0,1},{1,0},{2,3},{3,2},{4,5},{5,4},{6,7},{7,6},{8,9},{9,8},{10,11... | collective-permute-start | bytes 725000 | tf_op jit(solution)/shard_map/ppermute | solution.py:586
  56.2 3.2 %collective-permute-start.11 = (bf16[944,128]{1,0:T(8,128)(2,1)S(1)}, bf16[944,128]{1,0:T(8,128)(2,1)S(1)}, u32[]{:S(2)}, u32[]{:S(2)}) collective-permute-start(bf16[944,128]{1,0:T(8,128)(2,1)S(1)} %collective-permute-done.9.refs_7_), channel_id=1, source_target_pairs={{0,1},{1,0},{2,3},{3,2},{4,5},{5,4},{6,7},{7,6},{8,9},{9,8},{10,11... | collective-permute-start | bytes 725000 | tf_op jit(solution)/shard_map/ppermute | solution.py:586
  59.4 1.5 %collective-permute-start.12 = (bf16[944,128]{1,0:T(8,128)(2,1)S(1)}, bf16[944,128]{1,0:T(8,128)(2,1)S(1)}, u32[]{:S(2)}, u32[]{:S(2)}) collective-permute-start(bf16[944,128]{1,0:T(8,128)(2,1)S(1)} %collective-permute-done.7.refs_3_), channel_id=1, source_target_pairs={{0,1},{1,0},{2,3},{3,2},{4,5},{5,4},{6,7},{7,6},{8,9},{9,8},{10,11... | collective-permute-start | bytes 725000 | tf_op jit(solution)/shard_map/ppermute | solution.py:586
  70.4 2.3 %collective-permute-start.13 = (bf16[1232,128]{1,0:T(8,128)(2,1)S(1)}, bf16[1232,128]{1,0:T(8,128)(2,1)S(1)}, u32[]{:S(2)}, u32[]{:S(2)}) collective-permute-start(bf16[1232,128]{1,0:T(8,128)(2,1)S(1)} %get-tuple-element.84), channel_id=1, source_target_pairs={{0,1},{1,0},{2,3},{3,2},{4,5},{5,4},{6,7},{7,6},{8,9},{9,8},{10,11... | collective-permute-start | bytes 946184 | tf_op jit(solution)/shard_map/ppermute | solution.py:586
  72.2 3.4 %collective-permute-start.14 = (bf16[1232,128]{1,0:T(8,128)(2,1)S(1)}, bf16[1232,128]{1,0:T(8,128)(2,1)S(1)}, u32[]{:S(2)}, u32[]{:S(2)}) collective-permute-start(bf16[1232,128]{1,0:T(8,128)(2,1)S(1)} %get-tuple-element.87), channel_id=1, source_target_pairs={{0,1},{1,0},{2,3},{3,2},{4,5},{5,4},{6,7},{7,6},{8,9},{9,8},{10,11... | collective-permute-start | bytes 946184 | tf_op jit(solution)/shard_map/ppermute | solution.py:586
  72.8 12.7 %collective-permute-start.18 = (bf16[1232,128]{1,0:T(8,128)(2,1)S(1)}, bf16[1232,128]{1,0:T(8,128)(2,1)S(1)}, u32[]{:S(2)}, u32[]{:S(2)}) collective-permute-start(bf16[1232,128]{1,0:T(8,128)(2,1)S(1)} %add_convert_fusion.2), channel_id=1, source_target_pairs={{0,4},{1,5},{2,6},{3,7},{4,0},{5,1},{6,2},{7,3},{8,12},{9,13},{10,... | collective-permute-start | bytes 946184 | tf_op jit(solution)/shard_map/ppermute | solution.py:582
  75.3 4.5 %collective-permute-start.15 = (bf16[1232,128]{1,0:T(8,128)(2,1)S(1)}, bf16[1232,128]{1,0:T(8,128)(2,1)S(1)}, u32[]{:S(2)}, u32[]{:S(2)}) collective-permute-start(bf16[1232,128]{1,0:T(8,128)(2,1)S(1)} %get-tuple-element.93), channel_id=1, source_target_pairs={{0,1},{1,0},{2,3},{3,2},{4,5},{5,4},{6,7},{7,6},{8,9},{9,8},{10,11... | collective-permute-start | bytes 946184 | tf_op jit(solution)/shard_map/ppermute | solution.py:586
  75.7 14.2 %collective-permute-start.17 = (bf16[1232,128]{1,0:T(8,128)(2,1)S(1)}, bf16[1232,128]{1,0:T(8,128)(2,1)S(1)}, u32[]{:S(2)}, u32[]{:S(2)}) collective-permute-start(bf16[1232,128]{1,0:T(8,128)(2,1)S(1)} %add_convert_fusion.1), channel_id=1, source_target_pairs={{0,6},{1,7},{2,0},{3,1},{4,2},{5,3},{6,4},{7,5},{8,14},{9,15},{10,... | collective-permute-start | bytes 946184 | tf_op jit(solution)/shard_map/ppermute | solution.py:582
  79.5 10.3 %collective-permute-start.16 = (bf16[1232,128]{1,0:T(8,128)(2,1)S(1)}, bf16[1232,128]{1,0:T(8,128)(2,1)S(1)}, u32[]{:S(2)}, u32[]{:S(2)}) collective-permute-start(bf16[1232,128]{1,0:T(8,128)(2,1)S(1)} %get-tuple-element.100), channel_id=1, source_target_pairs={{0,1},{1,0},{2,3},{3,2},{4,5},{5,4},{6,7},{7,6},{8,9},{9,8},{10,11... | collective-permute-start | bytes 946184 | tf_op jit(solution)/shard_map/ppermute | solution.py:586
  79.9 11.0 %collective-permute-start.19 = (bf16[1232,128]{1,0:T(8,128)(2,1)S(1)}, bf16[1232,128]{1,0:T(8,128)(2,1)S(1)}, u32[]{:S(2)}, u32[]{:S(2)}) collective-permute-start(bf16[1232,128]{1,0:T(8,128)(2,1)S(1)} %add_convert_fusion), channel_id=1, source_target_pairs={{0,2},{1,3},{2,4},{3,5},{4,6},{5,7},{6,0},{7,1},{8,10},{9,11},{10,... | collective-permute-start | bytes 946184 | tf_op jit(solution)/shard_map/ppermute | solution.py:582
  (4 other events, 175.6 us)
